TPU v7x, 128 devices: a whole 4x4x4 slice. The times are simulated.
128 devices in a mesh: feed: 16 (over y, z_hi, core), tm: 8 (over z_lo, x).
Axes of the slice: x: 4, y: 4, z: 4 (z_hi: 2, z_lo: 2; z = z_hi * 2 + z_lo), core: 2. Of those that a mesh axis runs over, the one named last changes fastest.
Arguments:
- samples: int32 [512, 524288], P('feed', 'tm'), may hold values from -8 to 7
- input_map: int32 [512], replicated, may hold values from 0 to 511, each once
Outputs:
- visibility: float32 [1024, 2, 512, 512], P(('feed', 'tm'))
Inputs may be any that keep to these rules, and one draw needn't show every extreme that they name: `input_map`: each input appears once.
All inputs are finite; a program needn't handle non-finite values.
Results may differ from a plain program's by a relative error of at most 0.00055.
Values may be sent and summed in bfloat16 or wider, within the bound.
No kernel may reach another device: no remote copies, remote signals or barrier semaphores. Data moves between devices by JAX's collectives and lax.ppermute only.
A program may use at most 128 MiB of HBM per device.

v0:
```python
import math

import jax
import jax.numpy as jnp
from jax import lax
from jax.sharding import PartitionSpec as P

CHANNELS = 1024
NFFT = 2048
TAPS = 4


def from_behind(value, axis, steps):
    count = lax.axis_size(axis)
    initial, last = (max(0, -steps), min(count, count - steps))
    return lax.ppermute(value, axis, [(source, source + steps) for source in range(initial, last)])


def taper_table():
    total = TAPS * NFFT
    place = jnp.arange(total).astype(jnp.float32)
    offset = (place - (total - 1) / 2.0) / NFFT
    values = jnp.sinc(offset) * (0.54 - 0.46 * jnp.cos(2.0 * math.pi * place / (total - 1)))
    return values.reshape(TAPS, NFFT).astype(jnp.float32)


def transform_table():
    sample = jnp.arange(NFFT)[:, None]
    channel = jnp.arange(CHANNELS)[None, :]
    phase = (sample * channel % NFFT).astype(jnp.float32) * (2.0 * math.pi / NFFT)
    factor = (8.0 * NFFT) ** (-0.5)
    pair = jnp.stack([jnp.cos(phase) * factor, -jnp.sin(phase) * factor], axis=-1)
    return pair.reshape(NFFT, 2 * CHANNELS).astype(jnp.bfloat16)


def per_device(samples, input_map):
    feed_count = lax.axis_size("feed")
    time_count = lax.axis_size("tm")
    devices = feed_count * time_count
    local_rows = samples.shape[0]
    frames_dev = samples.shape[1] // NFFT
    wave = samples.astype(jnp.bfloat16)
    tail = wave[:, (frames_dev - (TAPS - 1)) * NFFT :]
    before = from_behind(tail, "tm", 1)
    extended = jnp.concatenate([before, wave], axis=1).reshape(
        local_rows, frames_dev + TAPS - 1, NFFT
    )
    taper = taper_table()
    filtered = jnp.zeros((local_rows, frames_dev, NFFT), jnp.float32)
    for tap in range(TAPS):
        filtered = filtered + taper[tap][None, None, :] * extended[
            :, tap : tap + frames_dev, :
        ].astype(jnp.float32)
    filtered = filtered.astype(jnp.bfloat16).reshape(local_rows * frames_dev, NFFT)
    spectra = lax.dot_general(
        transform_table(), filtered, (((0,), (1,)), ((), ())), preferred_element_type=jnp.float32
    )
    spectra = spectra.astype(jnp.bfloat16)
    chan_dev = CHANNELS // devices
    outgoing = spectra.reshape(devices, chan_dev, 2 * local_rows * frames_dev)
    incoming = lax.all_to_all(outgoing, ("feed", "tm"), split_axis=0, concat_axis=0, tiled=True)
    arranged = incoming.reshape(feed_count, time_count, chan_dev, 2, local_rows, frames_dev)
    arranged = arranged.transpose(2, 3, 0, 4, 1, 5).reshape(
        chan_dev, 2, feed_count * local_rows, time_count * frames_dev
    )
    ordered = jnp.take(arranged, input_map, axis=2)
    turned = jnp.stack([ordered[:, 1], -ordered[:, 0]], axis=1)
    paired = jnp.stack([ordered, turned], axis=1)
    norm = 1.0 / math.sqrt(time_count * frames_dev)
    result = jnp.einsum("corin,crjn->coij", paired, ordered, preferred_element_type=jnp.float32)
    return result * norm


def solution(mesh):
    in_specs = (P("feed", "tm"), P())
    out_specs = P(("feed", "tm"), None, None, None)
    return jax.shard_map(
        per_device, mesh=mesh, in_specs=in_specs, out_specs=out_specs, check_vma=False
    )
```

profile of v0, /device:TPU:1, one launch (start us, length us, event | category | flops | bytes accessed | tf_op | source)
XLA Modules:
  0.0 282.3 jit_solution(7652724277422525623)
XLA Ops:
  0.0 3.8 %convert_element_type.64 = bf16[32,65536]{1,0:T(8,128)(2,1)S(1)} convert(s32[32,65536]{1,0:T(8,128)} %param.2) | non-fusion elementwise | flops 2097152 | bytes 12582912 | tf_op jit(solution)/shard_map/convert_element_type | solution.py:42
  3.8 0.0 copy-start.1
  3.8 4.0 %collective-permute-start = (bf16[32,6144]{1,0:T(8,128)(2,1)S(1)}, bf16[32,6144]{1,0:T(8,128)(2,1)S(1)}, u32[]{:S(2)}, u32[]{:S(2)}) collective-permute-start(bf16[32,6144]{1,0:T(8,128)(2,1)S(1)} %slice.51), channel_id=1, source_target_pairs={{0,1},{1,2},{2,3},{3,4},{4,5},{5,6},{6,7},{8,9},{9,10},{10,11},{11... | collective-permute-start | bytes 1179656 | tf_op jit(solution)/shard_map/ppermute | solution.py:16
  7.8 34.9 %multiply_convert_fusion = (bf16[2048,1024,1]{1,0,2:T(8,128)(2,1)S(1)}, bf16[2048,1024,1]{1,0,2:T(8,128)(2,1)}) fusion(), kind=kLoop, calls=%fused_computation.13 | loop fusion | flops 39845888 | bytes 8388608 | tf_op jit(solution)/shard_map/convert.1
  42.7 0.0 copy-done.1
  42.7 6.3 %pad_maximum_fusion = bf16[2048,1024,2]{1,0,2:T(8,128)(2,1)} fusion(bf16[2048,1024,1]{1,0,2:T(8,128)(2,1)S(1)} %get-tuple-element.11, bf16[2048,1024,1]{1,0,2:T(8,128)(2,1)} %get-tuple-element.12), kind=kLoop, calls=%fused_computation.8 | loop fusion | flops 4194304 | bytes 16777216 | tf_op jit(solution)/shard_map/stack | solution.py:32
  49.0 21.5 %copy.11 = bf16[2048,1024,2]{0,2,1:T(2,128)(2,1)} copy(bf16[2048,1024,2]{1,0,2:T(8,128)(2,1)} %pad_maximum_fusion) | data formatting | bytes 16777216 | tf_op jit(solution)/shard_map/stack | solution.py:32
  70.5 13.0 %convert_element_type.62 = bf16[2048,2048]{0,1:T(8,128)(2,1)} reshape(bf16[2048,1024,2]{0,2,1:T(2,128)(2,1)} %copy.11) | data formatting | bytes 16777216 | tf_op jit(solution)/shard_map/convert_element_type | solution.py:33
  83.5 0.2 fusion.15
  83.7 0.0 collective-permute-done
  83.7 4.6 %pad_maximum_fusion.1 = bf16[32,71680]{1,0:T(8,128)(2,1)} fusion(bf16[32,65536]{1,0:T(8,128)(2,1)} %copy-done.1, bf16[32,6144]{1,0:T(8,128)(2,1)S(1)} %collective-permute-done), kind=kLoop, calls=%fused_computation.18 | loop fusion | flops 9175040 | bytes 9175040 | tf_op jit(solution)/shard_map/concatenate | solution.py:45
  88.4 6.2 %reshape.125 = bf16[32,35,2048]{2,1,0:T(8,128)(2,1)} reshape(bf16[32,71680]{1,0:T(8,128)(2,1)} %pad_maximum_fusion.1) | data formatting | bytes 9175040 | tf_op jit(solution)/shard_map/reshape | solution.py:45
  94.6 11.4 %add_convert_fusion = bf16[32,32,2048]{2,1,0:T(8,128)(2,1)S(1)} fusion(bf16[32,35,2048]{2,1,0:T(8,128)(2,1)} %reshape.125, f32[2048]{0:T(1024)S(1)} %get-tuple-element.8, f32[2048]{0:T(1024)S(1)} %get-tuple-element.9, f32[2048]{0:T(1024)S(1)} %get-tuple-element.10, f32[2048]{0:T(1024)S(1)} %get-tuple-element.7), kind=kLoop, calls=%fused_computation.12 | loop fusion | flops 25165824 | bytes 21004288 | tf_op jit(solution)/shard_map/convert_element_type | solution.py:54
  106.0 12.8 %convolution_convert_fusion = bf16[2048,1024]{1,0:T(8,128)(2,1)} fusion(bf16[2048,2048]{0,1:T(8,128)(2,1)} %convert_element_type.62, bf16[1024,2048]{1,0:T(8,128)(2,1)S(1)} %bitcast.30), kind=kOutput, calls=%fused_computation.24 | convolution fusion | flops 8592031744 | bytes 16777216 | tf_op jit(solution)/shard_map/dot_general | solution.py:55
  118.8 7.1 %reshape.127 = bf16[128,8,2048]{2,1,0:T(8,128)(2,1)} reshape(bf16[2048,1024]{1,0:T(8,128)(2,1)} %convolution_convert_fusion) | data formatting | bytes 8388608 | tf_op jit(solution)/shard_map/reshape | solution.py:60
  125.9 0.0 copy-start.3
  125.9 11.1 %all-to-all-start = ((bf16[128,8,2048]{2,1,0:T(8,128)(2,1)}), bf16[128,8,2048]{2,1,0:T(8,128)(2,1)}, u32[]{:S(2)}, u32[]{:S(2)}) async-start(bf16[128,8,2048]{2,1,0:T(8,128)(2,1)} %reshape.127), calls=%async_computation | async-start | bytes 8388608 | tf_op jit(solution)/shard_map/all_to_all | solution.py:61
  137.0 0.0 copy-done.3
  137.0 53.7 %all-to-all-done = bf16[128,8,2048]{2,1,0:T(8,128)(2,1)} async-done(((bf16[128,8,2048]{2,1,0:T(8,128)(2,1)}), bf16[128,8,2048]{2,1,0:T(8,128)(2,1)}, u32[]{:S(2)}, u32[]{:S(2)}) %all-to-all-start) | async-done | bytes 4194336 | tf_op jit(solution)/shard_map/all_to_all | solution.py:61
  190.7 19.4 %reshape.128 = bf16[16,8,8,2,32,32]{5,4,3,2,1,0:T(8,128)(2,1)} reshape(bf16[128,8,2048]{2,1,0:T(8,128)(2,1)} %all-to-all-done) | data formatting | bytes 8388608 | tf_op jit(solution)/shard_map/reshape | solution.py:62
  210.1 18.7 %copy.18 = bf16[8,2,16,32,8,32]{5,4,0,3,2,1:T(8,128)(2,1)} copy(bf16[8,2,16,32,8,32]{5,3,1,0,4,2:T(8,128)(2,1)} %bitcast.29) | data formatting | bytes 8388608 | tf_op jit(solution)/shard_map/reshape | solution.py:63
  228.8 20.3 %reshape.141 = bf16[8,2,512,256]{3,0,2,1:T(8,128)(2,1)} reshape(bf16[8,2,16,32,8,32]{5,4,0,3,2,1:T(8,128)(2,1)} %copy.18) | data formatting | bytes 8388608 | tf_op jit(solution)/shard_map/reshape | solution.py:63
  249.1 5.2 %gather_fusion = bf16[512,8,2,256]{3,1,2,0:T(8,128)(2,1)} fusion(bf16[8,2,512,256]{3,0,2,1:T(8,128)(2,1)} %reshape.141, s32[1024]{0:T(1024)S(1)} %pad_clamp_fusion), kind=kCustom, calls=%fused_computation | custom fusion | bytes 8390656 | tf_op jit(solution)/shard_map/jit(_take)/gather | solution.py:66
  254.4 0.0 copy-start
  254.4 5.2 %bitcast_select_fusion.1 = bf16[8,2,512,256]{3,2,1,0:T(8,128)(2,1)S(1)} fusion(pred[512]{0:T(512)(128)(4,1)S(1)} %compare_and_fusion, bf16[512,8,2,256]{3,1,2,0:T(8,128)(2,1)} %gather_fusion), kind=kLoop, calls=%fused_computation.23 | loop fusion | flops 2097152 | bytes 8389120 | tf_op jit(solution)/shard_map/jit(_take)/select_n | solution.py:66
  259.5 0.0 copy-done
  259.5 0.0 copy-start.2
  259.5 4.8 %fusion.10 = bf16[8,1,2,512,256]{4,3,2,1,0:T(8,128)(2,1)} fusion(pred[512]{0:T(512)(128)(4,1)S(1)} %compare_and_fusion, bf16[512,8,2,256]{3,1,2,0:T(8,128)(2,1)S(1)} %copy-done), kind=kLoop, calls=%fused_computation.22 | loop fusion | flops 2097152 | bytes 8389120 | tf_op jit(solution)/shard_map/jit(_take)/select_n | solution.py:66
  264.4 0.3 fusion.25
  264.6 0.0 copy-done.2
  264.7 2.3 maximum_bitcast_fusion
  267.0 15.4 %bitcast_multiply_fusion = f32[8,2,512,512]{3,2,1,0:T(8,128)} fusion(bf16[8,1,2,512,256]{4,3,2,1,0:T(8,128)(2,1)} %maximum_bitcast_fusion, bf16[8,1,2,512,256]{4,3,2,1,0:T(8,128)(2,1)} %fusion.10, bf16[8,2,512,256]{3,2,1,0:T(8,128)(2,1)} %copy-done.2), kind=kOutput, calls=%fused_computation.1 | convolution fusion | flops 4303355904 | bytes 29360128 | tf_op jit(solution)/shard_map/corin,crjn->coij/dot_general | solution.py:70
  (5 shorter events, 0.1 us)
Async XLA Ops:
  3.8 38.9 %copy-start.1 = (bf16[32,65536]{1,0:T(8,128)(2,1)}, bf16[32,65536]{1,0:T(8,128)(2,1)S(1)}, u32[]{:S(2)}) copy-start(bf16[32,65536]{1,0:T(8,128)(2,1)S(1)} %convert_element_type.64) | copy-start | bytes 12582916
  3.8 79.9 %collective-permute-start = (bf16[32,6144]{1,0:T(8,128)(2,1)S(1)}, bf16[32,6144]{1,0:T(8,128)(2,1)S(1)}, u32[]{:S(2)}, u32[]{:S(2)}) collective-permute-start(bf16[32,6144]{1,0:T(8,128)(2,1)S(1)} %slice.51), channel_id=1, source_target_pairs={{0,1},{1,2},{2,3},{3,4},{4,5},{5,6},{6,7},{8,9},{9,10},{10,11},{11... | collective-permute-start | bytes 1179656 | tf_op jit(solution)/shard_map/ppermute | solution.py:16
  125.9 11.1 %copy-start.3 = (s32[512]{0:T(512)S(1)}, s32[512]{0:T(512)}, u32[]{:S(2)}) copy-start(s32[512]{0:T(512)} %param.3) | copy-start | bytes 6148
  125.9 64.8 %all-to-all-start = ((bf16[128,8,2048]{2,1,0:T(8,128)(2,1)}), bf16[128,8,2048]{2,1,0:T(8,128)(2,1)}, u32[]{:S(2)}, u32[]{:S(2)}) async-start(bf16[128,8,2048]{2,1,0:T(8,128)(2,1)} %reshape.127), calls=%async_computation | async-start | bytes 8388608 | tf_op jit(solution)/shard_map/all_to_all | solution.py:61
  254.4 5.2 %copy-start = (bf16[512,8,2,256]{3,1,2,0:T(8,128)(2,1)S(1)}, bf16[512,8,2,256]{3,1,2,0:T(8,128)(2,1)}, u32[]{:S(2)}) copy-start(bf16[512,8,2,256]{3,1,2,0:T(8,128)(2,1)} %gather_fusion) | copy-start | bytes 12582916
  259.5 5.1 %copy-start.2 = (bf16[8,2,512,256]{3,2,1,0:T(8,128)(2,1)}, bf16[8,2,512,256]{3,2,1,0:T(8,128)(2,1)S(1)}, u32[]{:S(2)}) copy-start(bf16[8,2,512,256]{3,2,1,0:T(8,128)(2,1)S(1)} %bitcast_select_fusion.1) | copy-start | bytes 12582916
where the time goes:
time: 285 us; the launch traced here: 282 us
  local copies, waits for them, and re-layouts  112 us (39%)
  other arithmetic  73.8 us (26%)
  waiting for transfers between devices  53.7 us (19%)
  matrix products  28.1 us (10%)
  starting transfers between devices  15.1 us (5%)
    all_to_all x1, waiting for transfers between devices, per_device(): lax.all_to_all(outgoing, ('feed', 'tm'), split_axis=0, concat_axis=0, til...  53.7 us
    reshape x2, local copies, waits for them, and re-layouts, per_device(): arranged.transpose(2, 3, 0, 4, 1, 5)  39.1 us
    another operation x1, other arithmetic  34.9 us
    another operation x1, local copies, waits for them, and re-layouts, transform_table(): jnp.stack([jnp.cos(phase) * factor, -jnp.sin(phase) * factor], axis=-1)  21.5 us
    reshape x1, local copies, waits for them, and re-layouts, per_device(): incoming.reshape(feed_count, time_count, chan_dev, 2, local_rows, frames_...  19.4 us
    dot_general x1, matrix products, per_device(): jnp.einsum('corin,crjn->coij', paired, ordered, preferred_element_type=jn...  15.4 us
    convert_element_type x1, local copies, waits for them, and re-layouts, transform_table(): return pair.reshape(NFFT, 2 * CHANNELS).astype(jnp.bfloat16)  13 us
    dot_general x1, matrix products, per_device(): lax.dot_general(transform_table(), filtered, (((0,), (1,)), ((), ())), pr...  12.8 us
  transfers between devices with their start and end apart: 2, of which 1 were waited for; matrix products, arithmetic and copies ran while one was open for 27% of the time, Pallas kernels for 0%

commit v1 on v0

v1 whole, which is shorter than its diff:
```python
import functools
import math

import jax
import jax.numpy as jnp
import ml_dtypes
import numpy as np
from jax import lax
from jax.experimental import pallas as pl
from jax.experimental.pallas import tpu as pltpu
from jax.sharding import PartitionSpec as P

CHANNELS = 1024
NFFT = 2048
TAPS = 4
HALO = TAPS - 1
LANES = 128
GROUP = 8
TILE = 256
CHUNKS = (8,)
VMEM = 56 * 1024 * 1024


def taper_table():
    total = TAPS * NFFT
    place = np.arange(total).astype(np.float32)
    offset = (place - np.float32((total - 1) / 2.0)) / np.float32(NFFT)
    arg = np.float32(math.pi) * offset
    sinc = np.sin(arg) / arg
    window = np.float32(0.54) - np.float32(0.46) * np.cos(
        np.float32(2.0 * math.pi) * place / np.float32(total - 1)
    )
    return (sinc * window).astype(np.float32).reshape(TAPS, NFFT)


def transform_table(devices, first, count):
    per = CHANNELS // devices
    sample = np.arange(NFFT)[None, :]
    channel = (np.arange(devices)[:, None] * per + first + np.arange(count)[None, :]).reshape(-1, 1)
    phase = (sample * channel % NFFT).astype(np.float32) * np.float32(2.0 * math.pi / NFFT)
    factor = np.float32((8.0 * NFFT) ** (-0.5))
    pair = np.stack([np.cos(phase) * factor, -np.sin(phase) * factor], axis=1)
    return pair.reshape(2 * devices * count, NFFT).astype(ml_dtypes.bfloat16)


def filter_kernel(frames, samples_ref, halo_ref, taper_ref, out_ref, carry_ref):
    step = pl.program_id(0)

    @pl.when(step == 0)
    def _():
        carry_ref[...] = halo_ref[...].astype(jnp.float32)

    rows = samples_ref.shape[0]

    def columns(chunk, _):
        start = pl.multiple_of(chunk * LANES, LANES)
        taper = [taper_ref[tap, pl.ds(start, LANES)][None, :] for tap in range(TAPS)]
        for row in range(0, rows, 16):
            part = pl.ds(row, 16)
            x = [carry_ref[part, pl.ds(start + t * NFFT, LANES)] for t in range(HALO)]
            for k in range(frames):
                x.append(samples_ref[part, pl.ds(start + k * NFFT, LANES)].astype(jnp.float32))
                value = taper[0] * x[k]
                for tap in range(1, TAPS):
                    value = value + taper[tap] * x[k + tap]
                out_ref[pl.ds(k * rows + row, 16), pl.ds(start, LANES)] = value.astype(jnp.bfloat16)
            for t in range(HALO):
                carry_ref[part, pl.ds(start + t * NFFT, LANES)] = x[frames + t]
        return 0

    lax.fori_loop(0, NFFT // LANES, columns, 0)


def filtered_frames(samples, halo, taper):
    rows, length = samples.shape
    steps = length // (GROUP * NFFT)
    return pl.pallas_call(
        functools.partial(filter_kernel, GROUP),
        grid=(steps,),
        in_specs=[
            pl.BlockSpec((rows, GROUP * NFFT), lambda i: (0, i)),
            pl.BlockSpec((rows, HALO * NFFT), lambda i: (0, 0)),
            pl.BlockSpec((TAPS, NFFT), lambda i: (0, 0)),
        ],
        out_specs=pl.BlockSpec((GROUP * rows, NFFT), lambda i: (i, 0)),
        out_shape=jax.ShapeDtypeStruct((rows * length // NFFT, NFFT), jnp.bfloat16),
        scratch_shapes=[pltpu.VMEM((rows, HALO * NFFT), jnp.float32)],
        compiler_params=pltpu.CompilerParams(vmem_limit_bytes=VMEM),
        cost_estimate=pl.CostEstimate(
            flops=8 * rows * length, bytes_accessed=6 * rows * length, transcendentals=0
        ),
        name="filter",
    )(samples, halo, taper)


def transform_kernel(table_ref, filtered_ref, out_ref, turn_ref):
    value = lax.dot_general(
        table_ref[...],
        filtered_ref[...],
        (((1,), (1,)), ((), ())),
        preferred_element_type=jnp.float32,
    )
    count = value.shape[1] // LANES
    for j in range(count):
        turn_ref[pl.ds(j, value.shape[0], stride=count), :] = value[:, j * LANES : (j + 1) * LANES]
    out_ref[...] = turn_ref[...].astype(jnp.bfloat16).reshape(out_ref.shape)


def transformed(table, filtered, devices, count):
    total = filtered.shape[0]
    per = total // LANES
    rows = 2 * devices * count
    return pl.pallas_call(
        transform_kernel,
        grid=(rows // TILE,),
        in_specs=[
            pl.BlockSpec((TILE, NFFT), lambda i: (i, 0)),
            pl.BlockSpec((total, NFFT), lambda i: (0, 0)),
        ],
        out_specs=pl.BlockSpec(
            (TILE // (2 * count), count, 2 * per, LANES), lambda i: (i, 0, 0, 0)
        ),
        out_shape=jax.ShapeDtypeStruct((devices, count, 2 * per, LANES), jnp.bfloat16),
        scratch_shapes=[pltpu.VMEM((TILE * per, LANES), jnp.float32)],
        compiler_params=pltpu.CompilerParams(vmem_limit_bytes=VMEM),
        cost_estimate=pl.CostEstimate(
            flops=2 * rows * NFFT * total,
            bytes_accessed=2 * (rows * NFFT + total * NFFT + rows * total),
            transcendentals=0,
        ),
        name="transform",
    )(table, filtered)


def gram_kernel(feeds, times, norm, x_ref, place_ref, *refs):
    out_ref, turned_ref, z_ref = refs[-3:]
    per = x_ref.shape[2] // 2
    inputs = place_ref.shape[0]
    block = inputs // feeds
    inner = LANES // block
    high = times * per
    frames = inner * high
    for first in range(0, feeds, inner):
        parts = []
        for f in range(first, first + inner):
            x = x_ref[f * times : (f + 1) * times, 0].astype(jnp.float32)
            x = x.reshape(times, 2, per, LANES)
            parts.append([x[:, r].reshape(high, LANES) for r in range(2)])
        for r in range(2):
            for k in range(inner):
                side = jnp.concatenate(
                    [part[r][:, k * block : (k + 1) * block] for part in parts], axis=1
                )
                turned_ref[
                    r * frames + k * high : r * frames + (k + 1) * high,
                    first * block : (first + inner) * block,
                ] = side.astype(jnp.bfloat16)
    z = lax.dot_general(
        place_ref[...],
        turned_ref[...],
        (((1,), (1,)), ((), ())),
        preferred_element_type=jnp.float32,
    )
    z_ref[0] = z.astype(jnp.bfloat16)
    z_ref[1, :, :frames] = z[:, frames:].astype(jnp.bfloat16)
    z_ref[1, :, frames:] = (-z[:, :frames]).astype(jnp.bfloat16)
    for r in range(2):
        out_ref[0, r] = norm * lax.dot_general(
            z_ref[r], z_ref[0], (((1,), (1,)), ((), ())), preferred_element_type=jnp.float32
        )


def grams(incoming, place, previous, first, channels, feeds, times):
    count, per = incoming.shape[1], incoming.shape[2] // 2
    inputs = place.shape[0]
    frames = times * per * LANES * feeds // inputs
    in_specs = [
        pl.BlockSpec((feeds * times, 1, 2 * per, LANES), lambda c: (0, c, 0, 0)),
        pl.BlockSpec((inputs, inputs), lambda c: (0, 0)),
    ]
    args = [incoming, place]
    aliases = {}
    if previous is not None:
        in_specs.append(pl.BlockSpec(memory_space=pl.ANY))
        args.append(previous)
        aliases = {2: 0}
    return pl.pallas_call(
        functools.partial(gram_kernel, feeds, times, 1.0 / math.sqrt(frames)),
        grid=(count,),
        in_specs=in_specs,
        out_specs=pl.BlockSpec((1, 2, inputs, inputs), lambda c: (first + c, 0, 0, 0)),
        out_shape=jax.ShapeDtypeStruct((channels, 2, inputs, inputs), jnp.float32),
        scratch_shapes=[
            pltpu.VMEM((2 * frames, inputs), jnp.bfloat16),
            pltpu.VMEM((2, inputs, 2 * frames), jnp.bfloat16),
        ],
        input_output_aliases=aliases,
        compiler_params=pltpu.CompilerParams(vmem_limit_bytes=VMEM),
        cost_estimate=pl.CostEstimate(
            flops=count * 12 * inputs * inputs * frames,
            bytes_accessed=count * (8 * inputs * inputs + 4 * inputs * frames),
            transcendentals=0,
        ),
        name="gram",
    )(*args)


def per_device(samples, input_map):
    feeds = lax.axis_size("feed")
    times = lax.axis_size("tm")
    devices = feeds * times
    channels = CHANNELS // devices
    tail = samples[:, samples.shape[1] - HALO * NFFT :].astype(jnp.bfloat16)
    halo = lax.ppermute(tail, "tm", [(t, t + 1) for t in range(times - 1)])
    filtered = filtered_frames(samples, halo, jnp.asarray(taper_table()))
    inputs = input_map.shape[0]
    place = (input_map[:, None] == jnp.arange(inputs)[None, :]).astype(jnp.bfloat16)
    result = None
    first = 0
    arrived = []
    for count in CHUNKS:
        table = jnp.asarray(transform_table(devices, first, count))
        outgoing = transformed(table, filtered, devices, count)
        incoming = lax.all_to_all(
            outgoing, ("feed", "tm"), split_axis=0, concat_axis=0, tiled=True
        )
        arrived.append((first, incoming))
        first += count
    for first, incoming in arrived:
        result = grams(incoming, place, result, first, channels, feeds, times)
    return result


def solution(mesh):
    in_specs = (P("feed", "tm"), P())
    out_specs = P(("feed", "tm"), None, None, None)
    return jax.shard_map(
        per_device, mesh=mesh, in_specs=in_specs, out_specs=out_specs, check_vma=False
    )
```

time: 285 us -> 117 us (0.41)
  local copies, waits for them, and re-layouts: 112 us -> 0.75 us
  other arithmetic: 73.8 us -> 2.18 us
  Pallas kernels: 0 us -> 35.8 us
  matrix products: 28.1 us -> 0 us
  waiting for transfers between devices: 53.7 us -> 60.4 us
    reshape x5 -> x0, local copies, waits for them, and re-layouts: 71.7 us -> none  [the longest x2 39.1 us: per_device(): arranged.transpose(2, 3, 0, 4, 1, 5)]
    another operation x3 -> x1, other arithmetic: 43.5 us -> 1.17 us
    pallas_call x0 -> x3, Pallas kernels: none -> 35.8 us  [the longest x1 14.5 us: transformed(): pl.pallas_call(transform_kernel, grid=(rows // TILE,), in_specs=[pl.Block...]
    dot_general x2 -> x0, matrix products: 28.1 us -> none  [the longest x1 15.4 us: per_device(): jnp.einsum('corin,crjn->coij', paired, ordered, preferred_element_type=jn...]
    another operation x1 -> x0, local copies, waits for them, and re-layouts: 21.5 us -> none  [transform_table(): jnp.stack([jnp.cos(phase) * factor, -jnp.sin(phase) * factor], axis=-1)]
    convert_element_type x2 -> x1, other arithmetic: 15.2 us -> 1 us  [per_device(): (input_map[:, None] == jnp.arange(inputs)[None, :]).astype(jnp.bfloat16)]
    convert_element_type x1 -> x0, local copies, waits for them, and re-layouts: 13 us -> none  [transform_table(): return pair.reshape(NFFT, 2 * CHANNELS).astype(jnp.bfloat16)]
    select_n x3 -> x0, other arithmetic: 9.98 us -> none  [per_device(): ordered = jnp.take(arranged, input_map, axis=2)]
  transfers between devices with their start and end apart: 2 -> 2, of which waited for: 1 -> 2; matrix products, arithmetic and copies ran while one was open for 27% -> 1% of each run, Pallas kernels for 0% -> 0%
where the time goes in v1:
time: 117 us; the launch traced here: 116 us
  waiting for transfers between devices  60.4 us (52%)
  Pallas kernels  35.8 us (31%)
  starting transfers between devices  16.9 us (14%)
  other arithmetic  2.18 us (2%)
    all_to_all x1, waiting for transfers between devices, per_device(): lax.all_to_all(outgoing, ('feed', 'tm'), split_axis=0, concat_axis=0, til...  52.7 us
    pallas_call x1, Pallas kernels, transformed(): pl.pallas_call(transform_kernel, grid=(rows // TILE,), in_specs=[pl.Block...  14.5 us
    pallas_call x1, Pallas kernels, grams(): pl.pallas_call(functools.partial(gram_kernel, feeds, times, 1.0 / math.sq...  14 us
    all_to_all x1, starting transfers between devices, per_device(): lax.all_to_all(outgoing, ('feed', 'tm'), split_axis=0, concat_axis=0, til...  13 us
    ppermute x1, waiting for transfers between devices, per_device(): halo = lax.ppermute(tail, 'tm', [(t, t + 1) for t in range(times - 1)])  7.74 us
    pallas_call x1, Pallas kernels, filtered_frames(): pl.pallas_call(functools.partial(filter_kernel, GROUP), grid=(steps,), in...  7.29 us
    ppermute x1, starting transfers between devices, per_device(): halo = lax.ppermute(tail, 'tm', [(t, t + 1) for t in range(times - 1)])  3.97 us
  transfers between devices with their start and end apart: 2, of which 2 were waited for; matrix products, arithmetic and copies ran while one was open for 1% of the time, Pallas kernels for 0%

profile of v1, /device:TPU:1, one launch (start us, length us, event | category | flops | bytes accessed | tf_op | source)
XLA Modules:
  0.0 116.2 jit_solution(13636992688011006978)
XLA Ops:
  0.0 1.2 %slice_convert_fusion = bf16[32,6144]{1,0:T(8,128)(2,1)S(1)} fusion(s32[32,65536]{1,0:T(8,128)} %samples_ref.1), kind=kLoop, calls=%fused_computation.2 | loop fusion | flops 196608 | bytes 1179648 | tf_op jit(solution)/shard_map/convert
  1.2 4.0 %collective-permute-start = (bf16[32,6144]{1,0:T(8,128)(2,1)S(1)}, bf16[32,6144]{1,0:T(8,128)(2,1)S(1)}, u32[]{:S(2)}, u32[]{:S(2)}) collective-permute-start(bf16[32,6144]{1,0:T(8,128)(2,1)S(1)} %slice_convert_fusion), channel_id=1, source_target_pairs={{0,1},{1,2},{2,3},{3,4},{4,5},{5,6},{6,7},{8,9},{9,10},{10,11},{11... | collective-permute-start | bytes 1179656 | tf_op jit(solution)/shard_map/ppermute | solution.py:214
  5.2 7.7 %collective-permute-done.halo_ref = bf16[32,6144]{1,0:T(8,128)(2,1)S(1)} collective-permute-done((bf16[32,6144]{1,0:T(8,128)(2,1)S(1)}, bf16[32,6144]{1,0:T(8,128)(2,1)S(1)}, u32[]{:S(2)}, u32[]{:S(2)}) %collective-permute-start) | collective-permute-done | bytes 393248 | tf_op jit(solution)/shard_map/ppermute | solution.py:214
  12.9 0.0 copy-start
  12.9 0.7 copy-done
  13.6 7.3 %filter.1.filtered_ref = bf16[1024,2048]{1,0:T(8,128)(2,1)} custom-call(s32[32,65536]{1,0:T(8,128)} %samples_ref.1, bf16[32,6144]{1,0:T(8,128)(2,1)} %copy-done, f32[4,2048]{1,0:T(4,128)} %constant.4.clone.taper_ref), custom_call_target="tpu_custom_call" | custom-call | flops 16777216 | bytes 12582912 | tf_op jit(solution)/shard_map/filter/pallas_call | solution.py:77
  20.9 14.5 %transform.1 = bf16[128,8,16,128]{3,2,1,0:T(8,128)(2,1)} custom-call(bf16[2048,2048]{1,0:T(8,128)(2,1)} %constant.5.clone.table_ref, bf16[1024,2048]{1,0:T(8,128)(2,1)} %filter.1.filtered_ref), custom_call_target="tpu_custom_call" | custom-call | flops 8589934592 | bytes 16777216 | tf_op jit(solution)/shard_map/transform/pallas_call | solution.py:113
  35.4 0.0 copy-start.1
  35.4 13.0 %all-to-all-start = ((bf16[128,8,16,128]{3,2,1,0:T(8,128)(2,1)}), bf16[128,8,16,128]{3,2,1,0:T(8,128)(2,1)}, u32[]{:S(2)}, u32[]{:S(2)}) async-start(bf16[128,8,16,128]{3,2,1,0:T(8,128)(2,1)} %transform.1), calls=%async_computation | async-start | bytes 8388608 | tf_op jit(solution)/shard_map/all_to_all | solution.py:224
  48.4 0.0 copy-done.1
  48.4 1.0 fusion.place_ref
  49.4 52.7 %all-to-all-done.x_ref = bf16[128,8,16,128]{3,2,1,0:T(8,128)(2,1)} async-done(((bf16[128,8,16,128]{3,2,1,0:T(8,128)(2,1)}), bf16[128,8,16,128]{3,2,1,0:T(8,128)(2,1)}, u32[]{:S(2)}, u32[]{:S(2)}) %all-to-all-start) | async-done | bytes 4194336 | tf_op jit(solution)/shard_map/all_to_all | solution.py:224
  102.1 14.0 %gram.1 = f32[8,2,512,512]{3,2,1,0:T(8,128)} custom-call(bf16[128,8,16,128]{3,2,1,0:T(8,128)(2,1)} %all-to-all-done.x_ref, bf16[512,512]{1,0:T(8,128)(2,1)} %fusion.place_ref), custom_call_target="tpu_custom_call" | custom-call | flops 6442450944 | bytes 20971520 | tf_op jit(solution)/shard_map/gram/pallas_call | solution.py:187
Async XLA Ops:
  1.2 11.7 %collective-permute-start = (bf16[32,6144]{1,0:T(8,128)(2,1)S(1)}, bf16[32,6144]{1,0:T(8,128)(2,1)S(1)}, u32[]{:S(2)}, u32[]{:S(2)}) collective-permute-start(bf16[32,6144]{1,0:T(8,128)(2,1)S(1)} %slice_convert_fusion), channel_id=1, source_target_pairs={{0,1},{1,2},{2,3},{3,4},{4,5},{5,6},{6,7},{8,9},{9,10},{10,11},{11... | collective-permute-start | bytes 1179656 | tf_op jit(solution)/shard_map/ppermute | solution.py:214
  12.9 0.7 copy-start
  35.4 13.0 %copy-start.1 = (s32[512]{0:T(512)S(1)}, s32[512]{0:T(512)}, u32[]{:S(2)}) copy-start(s32[512]{0:T(512)} %param.5) | copy-start | bytes 6148
  35.4 66.7 %all-to-all-start = ((bf16[128,8,16,128]{3,2,1,0:T(8,128)(2,1)}), bf16[128,8,16,128]{3,2,1,0:T(8,128)(2,1)}, u32[]{:S(2)}, u32[]{:S(2)}) async-start(bf16[128,8,16,128]{3,2,1,0:T(8,128)(2,1)} %transform.1), calls=%async_computation | async-start | bytes 8388608 | tf_op jit(solution)/shard_map/all_to_all | solution.py:224

commit v2 on v0

v2 whole, which is shorter than its diff:
```python
import functools
import math

import jax
import jax.numpy as jnp
import ml_dtypes
import numpy as np
from jax import lax
from jax.experimental import pallas as pl
from jax.experimental.pallas import tpu as pltpu
from jax.sharding import PartitionSpec as P

CHANNELS = 1024
NFFT = 2048
TAPS = 4
HALO = TAPS - 1
LANES = 128
GROUP = 8
PAIR = 2
TILE = 1024
MIB = 1024 * 1024


def taper_table():
    total = TAPS * NFFT
    place = np.arange(total).astype(np.float32)
    offset = (place - np.float32((total - 1) / 2.0)) / np.float32(NFFT)
    arg = np.float32(math.pi) * offset
    sinc = np.sin(arg) / arg
    window = np.float32(0.54) - np.float32(0.46) * np.cos(
        np.float32(2.0 * math.pi) * place / np.float32(total - 1)
    )
    return (sinc * window).astype(np.float32).reshape(TAPS, NFFT)


def transform_table():
    sample = np.arange(NFFT)[None, :]
    channel = np.arange(CHANNELS)[:, None]
    phase = (sample * channel % NFFT).astype(np.float32) * np.float32(2.0 * math.pi / NFFT)
    factor = np.float32((8.0 * NFFT) ** (-0.5))
    pair = np.stack([np.cos(phase) * factor, -np.sin(phase) * factor], axis=1)
    return pair.reshape(2 * CHANNELS, NFFT).astype(ml_dtypes.bfloat16)


def filter_columns(samples_ref, past, taper_ref, out_ref, chunk, frames, carry_ref=None):
    rows = samples_ref.shape[0]
    start = pl.multiple_of(chunk * LANES, LANES)
    taper = [taper_ref[pl.ds(tap, 1), pl.ds(start, LANES)] for tap in range(TAPS)]
    for row in range(0, rows, 16):
        part = pl.ds(row, 16)
        x = [past(t, part, start) for t in range(HALO)]
        for k in range(frames):
            x.append(samples_ref[part, pl.ds(start + k * NFFT, LANES)].astype(jnp.float32))
            value = taper[0] * x[k]
            for tap in range(1, TAPS):
                value = value + taper[tap] * x[k + tap]
            out_ref[pl.ds(k * rows + row, 16), pl.ds(start, LANES)] = value.astype(jnp.bfloat16)
        if carry_ref is not None:
            for t in range(HALO):
                carry_ref[part, pl.ds(start + t * NFFT, LANES)] = x[frames + t]


def transform_tile(table, filtered, turn_ref):
    value = lax.dot_general(
        table, filtered, (((1,), (1,)), ((), ())), preferred_element_type=jnp.float32
    )
    count = value.shape[1] // LANES
    for j in range(count):
        turn_ref[pl.ds(j, value.shape[0], stride=count), :] = value[:, j * LANES : (j + 1) * LANES]
    return turn_ref[...].astype(jnp.bfloat16)


def head_kernel(
    samples_ref, before_ref, taper_ref, table_ref, out_ref, first_ref,
    held_ref, carry_ref, even_ref, odd_ref, turn_ref, sems,
):
    step = pl.program_id(0)
    tiles = table_ref.shape[0] // TILE
    share = NFFT // LANES // tiles
    devices = out_ref.shape[0] // tiles

    def fetch(m):
        part = pl.ds(m * TILE, TILE)
        return pltpu.make_async_copy(table_ref.at[part], held_ref.at[part], sems.at[m])

    def past(t, part, start):
        return carry_ref[part, pl.ds(start + t * NFFT, LANES)]

    def past_first(t, part, start):
        lanes = pl.ds(start + (t + 1) * NFFT, LANES)
        return before_ref[part, lanes].astype(jnp.float32)

    @pl.when(step == 0)
    def _():
        for m in range(tiles):
            fetch(m).start()

        def body(m, _):
            for n in range(share):
                filter_columns(
                    samples_ref, past_first, taper_ref, even_ref, m * share + n, GROUP, carry_ref
                )
            return 0

        lax.fori_loop(0, tiles, body, 0)

    def both(now_ref, next_ref, wait):
        def body(m, _):
            if wait:
                fetch(m).wait()
            row = pl.multiple_of(m * TILE, TILE)
            tile = transform_tile(held_ref[pl.ds(row, TILE), :], now_ref[...], turn_ref)
            out_ref[pl.ds(m * devices, devices)] = tile.reshape((devices,) + out_ref.shape[1:])
            for n in range(share):
                filter_columns(
                    samples_ref, past, taper_ref, next_ref, m * share + n, GROUP, carry_ref
                )
            return 0

        lax.fori_loop(0, tiles, body, 0)

    pl.when(step == 1)(lambda: both(even_ref, odd_ref, True))
    pl.when(step == 2)(lambda: both(odd_ref, even_ref, False))
    pl.when(step == 3)(lambda: both(even_ref, first_ref, False))


def head(samples, taper, table, devices):
    rows, length = samples.shape
    groups = length // (GROUP * NFFT)
    assert groups == 4
    pairs = CHANNELS // devices // PAIR
    sub = PAIR * 2 * GROUP * rows // (LANES * PAIR * 2) * PAIR * 2
    spectra = (devices, pairs, groups, sub, LANES)
    width = GROUP * rows
    return pl.pallas_call(
        head_kernel,
        grid=(groups,),
        in_specs=[
            pl.BlockSpec((rows, GROUP * NFFT), lambda s: (0, (s + 1) % groups)),
            pl.BlockSpec((rows, 4 * NFFT), lambda s: (0, 1)),
            pl.BlockSpec((TAPS, NFFT), lambda s: (0, 0)),
            pl.BlockSpec(memory_space=pl.ANY),
        ],
        out_specs=[
            pl.BlockSpec(
                (devices, pairs, None, sub, LANES), lambda s: (0, 0, jnp.maximum(s, 1), 0, 0)
            ),
            pl.BlockSpec((width, NFFT), lambda s: (0, 0)),
        ],
        out_shape=[
            jax.ShapeDtypeStruct(spectra, jnp.bfloat16),
            jax.ShapeDtypeStruct((width, NFFT), jnp.bfloat16),
        ],
        scratch_shapes=[
            pltpu.VMEM(table.shape, jnp.bfloat16),
            pltpu.VMEM((rows, HALO * NFFT), jnp.float32),
            pltpu.VMEM((width, NFFT), jnp.bfloat16),
            pltpu.VMEM((width, NFFT), jnp.bfloat16),
            pltpu.VMEM((TILE * width // LANES, LANES), jnp.float32),
            pltpu.SemaphoreType.DMA((table.shape[0] // TILE,)),
        ],
        compiler_params=pltpu.CompilerParams(vmem_limit_bytes=60 * MIB),
        cost_estimate=pl.CostEstimate(
            flops=2 * table.shape[0] * NFFT * width * 3,
            bytes_accessed=2 * table.shape[0] * NFFT + 4 * rows * length,
            transcendentals=0,
        ),
        name="head",
    )(samples, samples, taper, table)


def tail_kernel(
    samples_ref, halo_ref, first_ref, taper_ref, table_ref, _, out_ref, filtered_ref, turn_ref
):
    rows = samples_ref.shape[0]

    @pl.when(pl.program_id(0) == 0)
    def _():
        keep = HALO * rows
        filtered_ref[keep:, :] = first_ref[keep:, :]

        def past(t, part, start):
            return halo_ref[part, pl.ds(start + t * NFFT, LANES)].astype(jnp.float32)

        def body(chunk, _):
            filter_columns(samples_ref, past, taper_ref, filtered_ref, chunk, HALO)
            return 0

        lax.fori_loop(0, NFFT // LANES, body, 0)

    tile = transform_tile(table_ref[...], filtered_ref[...], turn_ref)
    out_ref[...] = tile.reshape(out_ref.shape)


def tail(samples, halo, first, taper, table, spectra):
    rows = samples.shape[0]
    width = GROUP * rows
    devices, pairs, groups, sub, _ = spectra.shape
    tiles = table.shape[0] // TILE
    return pl.pallas_call(
        tail_kernel,
        grid=(tiles,),
        in_specs=[
            pl.BlockSpec((rows, HALO * NFFT), lambda m: (0, 0)),
            pl.BlockSpec((rows, HALO * NFFT), lambda m: (0, 0)),
            pl.BlockSpec((width, NFFT), lambda m: (0, 0)),
            pl.BlockSpec((TAPS, NFFT), lambda m: (0, 0)),
            pl.BlockSpec((TILE, NFFT), lambda m: (m, 0)),
            pl.BlockSpec(memory_space=pl.ANY),
        ],
        out_specs=pl.BlockSpec(
            (devices // tiles, pairs, None, sub, LANES), lambda m: (m, 0, 0, 0, 0)
        ),
        out_shape=jax.ShapeDtypeStruct(spectra.shape, spectra.dtype),
        scratch_shapes=[
            pltpu.VMEM((width, NFFT), jnp.bfloat16),
            pltpu.VMEM((TILE * width // LANES, LANES), jnp.float32),
        ],
        input_output_aliases={5: 0},
        compiler_params=pltpu.CompilerParams(vmem_limit_bytes=60 * MIB),
        cost_estimate=pl.CostEstimate(
            flops=2 * table.shape[0] * NFFT * width,
            bytes_accessed=2 * table.shape[0] * NFFT,
            transcendentals=0,
        ),
        name="tail",
    )(samples, halo, first, taper, table, spectra)


def lane_turn(parts, block):
    lane = lax.broadcasted_iota(jnp.int32, parts[0].shape, 1)
    for step in (2, 1):
        upper = (lane // (block * step)) % 2 == 1
        turned = list(parts)
        for p in range(4):
            if p & step:
                continue
            low, high = parts[p], parts[p + step]
            turned[p] = jnp.where(upper, pltpu.roll(high, step * block, 1), low)
            turned[p + step] = jnp.where(upper, high, pltpu.roll(low, LANES - step * block, 1))
        parts = turned
    return parts


def spread(x, wide_ref):
    wide_ref[...] = x.astype(jnp.float32).reshape(wide_ref.shape)


def arrange(wide_ref, turned_ref, channel, feeds):
    each = wide_ref.shape[0] // feeds
    high = each // 8
    block = turned_ref.shape[1] // feeds
    inner = LANES // block
    half = turned_ref.shape[0] // 2
    for first in range(0, feeds, inner):
        for r in range(2):
            parts = []
            for f in range(first, first + inner):
                start = f * each + 4 * channel + 2 * r
                both = [wide_ref[pl.ds(start + j, high, stride=8), :] for j in range(2)]
                parts.append(jnp.concatenate(both, axis=0).astype(jnp.bfloat16))
            for k, side in enumerate(lane_turn(parts, block)):
                row = r * half + 2 * k * high
                turned_ref[row : row + 2 * high, first * block : (first + inner) * block] = side


def product(a, b):
    return lax.dot_general(a, b, (((1,), (1,)), ((), ())), preferred_element_type=jnp.float32)


def order(turned_ref, place_ref, z_ref):
    inputs = place_ref.shape[0]
    frames = turned_ref.shape[0] // 2
    z = product(place_ref[...], turned_ref[...])
    z_ref[:inputs] = z.astype(jnp.bfloat16)
    z_ref[inputs:, :frames] = z[:, frames:].astype(jnp.bfloat16)
    z_ref[inputs:, frames:] = (-z[:, :frames]).astype(jnp.bfloat16)


def correlate(z_ref, out_ref, norm):
    inputs = z_ref.shape[1]
    value = norm * product(z_ref[...], z_ref[:inputs])
    out_ref[0] = value[:inputs]
    out_ref[1] = value[inputs:]


def gram_kernel(
    feeds, norm, x_ref, place_ref, out_ref, held_ref, wide_ref, turned0_ref, turned1_ref,
    z0_ref, z1_ref, done0_ref, done1_ref, in_sems, out_sems,
):
    turned, z, done = (turned0_ref, turned1_ref), (z0_ref, z1_ref), (done0_ref, done1_ref)
    pairs = x_ref.shape[1]

    def fetch(pair):
        return pltpu.make_async_copy(x_ref.at[:, pair], held_ref.at[pair], in_sems.at[pair])

    def send(channel, parity):
        return pltpu.make_async_copy(done[parity], out_ref.at[channel], out_sems.at[parity])

    def phase(pair, parity, third=True, second=True, first=True, wait=True):
        channel = PAIR * pair + parity
        if first and parity == 0:
            fetch(pair).wait()
        if third:
            if wait:
                send(channel - 4, parity).wait()
            correlate(z[parity], done[parity], norm)
        if second:
            order(turned[1 - parity], place_ref, z[1 - parity])
        if first:
            if parity == 0:
                spread(held_ref[pair], wide_ref)
            arrange(wide_ref, turned[parity], parity, feeds)
        if third:
            send(channel - 2, parity).start()

    for pair in range(pairs):
        fetch(pair).start()
    phase(0, 0, third=False, second=False)
    phase(0, 1, third=False)
    phase(1, 0, wait=False)
    phase(1, 1, wait=False)

    def body(pair, _):
        phase(pair, 0)
        phase(pair, 1)
        return 0

    lax.fori_loop(2, pairs, body, 0)
    phase(pairs, 0, first=False)
    phase(pairs, 1, second=False, first=False)
    for parity in range(PAIR):
        send(PAIR * pairs - 2 + parity, parity).wait()


def grams(incoming, place, feeds):
    devices, pairs, groups, sub, _ = incoming.shape
    channels = PAIR * pairs
    inputs = place.shape[0]
    frames = devices * groups * sub * LANES // (2 * PAIR * inputs)
    return pl.pallas_call(
        functools.partial(gram_kernel, feeds, 1.0 / math.sqrt(frames)),
        in_specs=[
            pl.BlockSpec(memory_space=pl.ANY),
            pl.BlockSpec(memory_space=pltpu.VMEM),
        ],
        out_specs=pl.BlockSpec(memory_space=pl.ANY),
        out_shape=jax.ShapeDtypeStruct((channels, 2, inputs, inputs), jnp.float32),
        scratch_shapes=[
            pltpu.VMEM((pairs, devices, groups, sub, LANES), jnp.bfloat16),
            pltpu.VMEM((devices * groups * sub, LANES), jnp.float32),
            pltpu.VMEM((2 * frames, inputs), jnp.bfloat16),
            pltpu.VMEM((2 * frames, inputs), jnp.bfloat16),
            pltpu.VMEM((2 * inputs, 2 * frames), jnp.bfloat16),
            pltpu.VMEM((2 * inputs, 2 * frames), jnp.bfloat16),
            pltpu.VMEM((2, inputs, inputs), jnp.float32),
            pltpu.VMEM((2, inputs, inputs), jnp.float32),
            pltpu.SemaphoreType.DMA((pairs,)),
            pltpu.SemaphoreType.DMA((PAIR,)),
        ],
        compiler_params=pltpu.CompilerParams(vmem_limit_bytes=60 * MIB),
        cost_estimate=pl.CostEstimate(
            flops=channels * 12 * inputs * inputs * frames,
            bytes_accessed=channels * (8 * inputs * inputs + 4 * inputs * frames),
            transcendentals=0,
        ),
        name="gram",
    )(incoming, place)


def per_device(samples, input_map):
    feeds = lax.axis_size("feed")
    times = lax.axis_size("tm")
    devices = feeds * times
    inputs = input_map.shape[0]
    taper = jnp.asarray(taper_table())
    table = jnp.asarray(transform_table())
    last = samples[:, samples.shape[1] - HALO * NFFT :].astype(jnp.bfloat16)
    halo = lax.ppermute(last, "tm", [(t, t + 1) for t in range(times - 1)])
    place = (input_map[:, None] == jnp.arange(inputs)[None, :]).astype(jnp.bfloat16)
    spectra, first = head(samples, taper, table, devices)
    outgoing = tail(samples, halo, first, taper, table, spectra)
    incoming = lax.all_to_all(outgoing, ("feed", "tm"), split_axis=0, concat_axis=0, tiled=True)
    return grams(incoming, place, feeds)


def solution(mesh):
    in_specs = (P("feed", "tm"), P())
    out_specs = P(("feed", "tm"), None, None, None)
    return jax.shard_map(
        per_device, mesh=mesh, in_specs=in_specs, out_specs=out_specs, check_vma=False
    )
```

time: 285 us -> 107 us (0.38)
  local copies, waits for them, and re-layouts: 112 us -> 0.76 us
  other arithmetic: 73.8 us -> 2.14 us
  Pallas kernels: 0 us -> 35.8 us
  matrix products: 28.1 us -> 0 us
    reshape x5 -> x0, local copies, waits for them, and re-layouts: 71.7 us -> none  [the longest x2 39.1 us: per_device(): arranged.transpose(2, 3, 0, 4, 1, 5)]
    another operation x3 -> x1, other arithmetic: 43.5 us -> 1.17 us
    pallas_call x0 -> x3, Pallas kernels: none -> 35.8 us  [the longest x1 15.8 us: head(): pl.pallas_call(head_kernel, grid=(groups,), in_specs=[pl.BlockSpec((rows,...]
    dot_general x2 -> x0, matrix products: 28.1 us -> none  [the longest x1 15.4 us: per_device(): jnp.einsum('corin,crjn->coij', paired, ordered, preferred_element_type=jn...]
    another operation x1 -> x0, local copies, waits for them, and re-layouts: 21.5 us -> none  [transform_table(): jnp.stack([jnp.cos(phase) * factor, -jnp.sin(phase) * factor], axis=-1)]
    convert_element_type x2 -> x1, other arithmetic: 15.2 us -> 0.96 us  [per_device(): (input_map[:, None] == jnp.arange(inputs)[None, :]).astype(jnp.bfloat16)]
    convert_element_type x1 -> x0, local copies, waits for them, and re-layouts: 13 us -> none  [transform_table(): return pair.reshape(NFFT, 2 * CHANNELS).astype(jnp.bfloat16)]
    select_n x3 -> x0, other arithmetic: 9.98 us -> none  [per_device(): ordered = jnp.take(arranged, input_map, axis=2)]
  transfers between devices with their start and end apart: 2 -> 2, of which waited for: 1 -> 1; matrix products, arithmetic and copies ran while one was open for 27% -> 1% of each run, Pallas kernels for 0% -> 15%
where the time goes in v2:
time: 107 us
  waiting for transfers between devices  52.7 us (49%)
  Pallas kernels  35.8 us (33%)
  starting transfers between devices  15.1 us (14%)
  other arithmetic  2.14 us (2%)
    all_to_all x1, waiting for transfers between devices, per_device(): lax.all_to_all(outgoing, ('feed', 'tm'), split_axis=0, concat_axis=0, til...  52.7 us
    pallas_call x1, Pallas kernels, head(): pl.pallas_call(head_kernel, grid=(groups,), in_specs=[pl.BlockSpec((rows,...  15.8 us
    pallas_call x1, Pallas kernels, grams(): pl.pallas_call(functools.partial(gram_kernel, feeds, 1.0 / math.sqrt(fram...  13.2 us
    all_to_all x1, starting transfers between devices, per_device(): lax.all_to_all(outgoing, ('feed', 'tm'), split_axis=0, concat_axis=0, til...  11.1 us
    pallas_call x1, Pallas kernels, tail(): pl.pallas_call(tail_kernel, grid=(tiles,), in_specs=[pl.BlockSpec((rows,...  6.91 us
    ppermute x1, starting transfers between devices, per_device(): halo = lax.ppermute(last, 'tm', [(t, t + 1) for t in range(times - 1)])  3.97 us
  transfers between devices with their start and end apart: 2, of which 1 were waited for; matrix products, arithmetic and copies ran while one was open for 1% of the time, Pallas kernels for 15%

profile of v2, /device:TPU:1, one launch (start us, length us, event | category | flops | bytes accessed | tf_op | source)
XLA Modules:
  0.0 106.6 jit_solution(5049156287399347245)
XLA Ops:
  0.0 1.2 %slice_convert_fusion = bf16[32,6144]{1,0:T(8,128)(2,1)S(1)} fusion(s32[32,65536]{1,0:T(8,128)} %samples_ref.3), kind=kLoop, calls=%fused_computation.2 | loop fusion | flops 196608 | bytes 1179648 | tf_op jit(solution)/shard_map/convert
  1.2 4.0 %collective-permute-start = (bf16[32,6144]{1,0:T(8,128)(2,1)S(1)}, bf16[32,6144]{1,0:T(8,128)(2,1)S(1)}, u32[]{:S(2)}, u32[]{:S(2)}) collective-permute-start(bf16[32,6144]{1,0:T(8,128)(2,1)S(1)} %slice_convert_fusion), channel_id=1, source_target_pairs={{0,1},{1,2},{2,3},{3,4},{4,5},{5,6},{6,7},{8,9},{9,10},{10,11},{11... | collective-permute-start | bytes 1179656 | tf_op jit(solution)/shard_map/ppermute | solution.py:379
  5.2 15.8 %head.1 = (bf16[128,4,4,8,128]{4,3,2,1,0:T(8,128)(2,1)}, bf16[256,2048]{1,0:T(8,128)(2,1)}) custom-call(s32[32,65536]{1,0:T(8,128)} %samples_ref.3, s32[32,65536]{1,0:T(8,128)} %samples_ref.3, f32[4,2048]{1,0:T(4,128)} %constant.4.clone.taper_ref, bf16[2048,2048]{1,0:T(8,128)(2,1)} %constant.5.clone.table_ref), custom_call_target="tpu_custom_call" | custom-call | flops 6442450944 | bytes 16777216 | tf_op jit(solution)/shard_map/head/pallas_call | solution.py:135
  20.9 0.0 collective-permute-done.halo_ref
  20.9 0.0 copy-start
  20.9 0.8 copy-done
  21.7 6.9 %tail.1 = bf16[128,4,4,8,128]{4,3,2,1,0:T(8,128)(2,1)} custom-call(s32[32,65536]{1,0:T(8,128)} %samples_ref.3, bf16[32,6144]{1,0:T(8,128)(2,1)} %copy-done, bf16[256,2048]{1,0:T(8,128)(2,1)} %get-tuple-element.7.first_ref, f32[4,2048]{1,0:T(4,128)} %constant.4.clone.taper_ref, ...), custom_call_target="tpu_custom_call", output_to_operand_aliasing={{}: (5, {})} | custom-call | flops 2147483648 | bytes 8388608 | tf_op jit(solution)/shard_map/tail/pallas_call | solution.py:200
  28.6 0.0 copy-start.1
  28.6 11.1 %all-to-all-start = ((bf16[128,4,4,8,128]{4,3,2,1,0:T(8,128)(2,1)}), bf16[128,4,4,8,128]{4,3,2,1,0:T(8,128)(2,1)}, u32[]{:S(2)}, u32[]{:S(2)}) async-start(bf16[128,4,4,8,128]{4,3,2,1,0:T(8,128)(2,1)} %tail.1), calls=%async_computation | async-start | bytes 8388608 | tf_op jit(solution)/shard_map/all_to_all | solution.py:383
  39.7 0.0 copy-done.1
  39.8 1.0 fusion.place_ref
  40.7 52.7 %all-to-all-done.x_ref = bf16[128,4,4,8,128]{4,3,2,1,0:T(8,128)(2,1)} async-done(((bf16[128,4,4,8,128]{4,3,2,1,0:T(8,128)(2,1)}), bf16[128,4,4,8,128]{4,3,2,1,0:T(8,128)(2,1)}, u32[]{:S(2)}, u32[]{:S(2)}) %all-to-all-start) | async-done | bytes 4194336 | tf_op jit(solution)/shard_map/all_to_all | solution.py:383
  93.4 13.2 %gram.1 = f32[8,2,512,512]{3,2,1,0:T(8,128)} custom-call(bf16[128,4,4,8,128]{4,3,2,1,0:T(8,128)(2,1)} %all-to-all-done.x_ref, bf16[512,512]{1,0:T(8,128)(2,1)} %fusion.place_ref), custom_call_target="tpu_custom_call" | custom-call | flops 6442450944 | bytes 20971520 | tf_op jit(solution)/shard_map/gram/pallas_call | solution.py:341
Async XLA Ops:
  1.2 19.8 %collective-permute-start = (bf16[32,6144]{1,0:T(8,128)(2,1)S(1)}, bf16[32,6144]{1,0:T(8,128)(2,1)S(1)}, u32[]{:S(2)}, u32[]{:S(2)}) collective-permute-start(bf16[32,6144]{1,0:T(8,128)(2,1)S(1)} %slice_convert_fusion), channel_id=1, source_target_pairs={{0,1},{1,2},{2,3},{3,4},{4,5},{5,6},{6,7},{8,9},{9,10},{10,11},{11... | collective-permute-start | bytes 1179656 | tf_op jit(solution)/shard_map/ppermute | solution.py:379
  20.9 0.8 copy-start
  28.6 11.1 %copy-start.1 = (s32[512]{0:T(512)S(1)}, s32[512]{0:T(512)}, u32[]{:S(2)}) copy-start(s32[512]{0:T(512)} %param.5) | copy-start | bytes 6148
  28.6 64.8 %all-to-all-start = ((bf16[128,4,4,8,128]{4,3,2,1,0:T(8,128)(2,1)}), bf16[128,4,4,8,128]{4,3,2,1,0:T(8,128)(2,1)}, u32[]{:S(2)}, u32[]{:S(2)}) async-start(bf16[128,4,4,8,128]{4,3,2,1,0:T(8,128)(2,1)} %tail.1), calls=%async_computation | async-start | bytes 8388608 | tf_op jit(solution)/shard_map/all_to_all | solution.py:383

commit v3 on v2

v3 whole, which is shorter than its diff:
```python
import functools
import math

import jax
import jax.numpy as jnp
import ml_dtypes
import numpy as np
from jax import lax
from jax.experimental import pallas as pl
from jax.experimental.pallas import tpu as pltpu
from jax.sharding import PartitionSpec as P

CHANNELS = 1024
NFFT = 2048
HALF = NFFT // 2
TAPS = 4
HALO = TAPS - 1
LANES = 128
GROUP = 8
PAIR = 2
SLOTS = (0, 4, 1, 7, 2, 6, 3, 5)
EXTRA = 16
PARTS = (528, 512)
MIB = 1024 * 1024


def sample_order():
    chunk = 2 * LANES * np.arange(HALF // LANES)[:, None]
    lane = np.arange(LANES)[None, :]
    even = chunk + 2 * lane
    odd = chunk + (LANES + 2 * lane) % (2 * LANES) + 1
    return np.concatenate([even.reshape(-1), odd.reshape(-1)])


def taper_table():
    total = TAPS * NFFT
    place = np.arange(total).astype(np.float32)
    offset = (place - np.float32((total - 1) / 2.0)) / np.float32(NFFT)
    arg = np.float32(math.pi) * offset
    sinc = np.sin(arg) / arg
    window = np.float32(0.54) - np.float32(0.46) * np.cos(
        np.float32(2.0 * math.pi) * place / np.float32(total - 1)
    )
    return (sinc * window).astype(np.float32).reshape(TAPS, NFFT)[:, sample_order()]


def transform_table(devices):
    per = CHANNELS // devices
    slots = np.array([per if slot == 0 else slot for slot in SLOTS])
    channel = (per * np.arange(devices // 2)[:, None] + slots[None, :]).reshape(-1)
    channel = np.concatenate([np.zeros(EXTRA // 2, np.int64), channel])
    phase = (channel[:, None] * sample_order()[None, :] % NFFT).astype(np.float32)
    phase = phase * np.float32(2.0 * math.pi / NFFT)
    factor = np.float32((8.0 * NFFT) ** (-0.5))
    pair = np.stack([np.cos(phase) * factor, -np.sin(phase) * factor], axis=1)
    return pair.reshape(-1, NFFT).astype(ml_dtypes.bfloat16)


def separate(left, right):
    lane = lax.broadcasted_iota(jnp.int32, left.shape, 1)
    low = lane < LANES // 2
    even_first = jnp.where(low, 2 * lane, 2 * lane - LANES + 1)
    odd_first = jnp.where(low, 2 * lane + 1, 2 * lane - LANES)
    left = jnp.take_along_axis(left, even_first, axis=1, mode="promise_in_bounds")
    right = jnp.take_along_axis(right, odd_first, axis=1, mode="promise_in_bounds")
    return jnp.where(low, left, right), jnp.where(low, right, left)


def frame_part(ref, part, frame, chunk):
    both = []
    for side in range(2):
        start = frame * NFFT + (2 * chunk + side) * LANES
        both.append(ref[part, start : start + LANES].astype(jnp.float32))
    return separate(*both)


def filter_chunk(ref, first, frames, taper_ref, out_ref, chunk, past, keep=None):
    rows = ref.shape[0]
    lanes = [slice(side * HALF + chunk * LANES, side * HALF + (chunk + 1) * LANES) for side in range(2)]
    taper = [[taper_ref[tap : tap + 1, lane] for tap in range(TAPS)] for lane in lanes]
    for row in range(0, rows, 16):
        part = slice(row, row + 16)
        x = [past(t, part, chunk) for t in range(HALO)]
        for k in range(frames):
            x.append(frame_part(ref, part, first + k, chunk))
            for side in range(2):
                value = taper[side][0] * x[k][side]
                for tap in range(1, TAPS):
                    value = value + taper[side][tap] * x[k + tap][side]
                place = (first + k) % GROUP * rows + row
                out_ref[place : place + 16, lanes[side]] = value.astype(jnp.bfloat16)
        if keep is not None:
            for t in range(HALO):
                keep(t, part, chunk, x[frames + t])


def transform_part(table_ref, filtered_ref, plus_ref, minus_ref, first, count):
    even, odd = (
        product(table_ref[first : first + count, lanes], filtered_ref[:, lanes])
        for lanes in (slice(0, HALF), slice(HALF, NFFT))
    )
    row = lax.broadcasted_iota(jnp.int32, (count, LANES), 0)
    sign = jnp.where(row % 2 == 0, 1.0, -1.0)
    total = even.shape[1] // LANES
    for j in range(total):
        e, o = (value[:, j * LANES : (j + 1) * LANES] for value in (even, odd))
        plus_ref[pl.ds(first * total + j, count, stride=total), :] = e + o
        minus_ref[pl.ds(first * total + j, count, stride=total), :] = sign * (e - o)


def pack(plus_ref, minus_ref, out_ref):
    devices, pairs, sub, _ = out_ref.shape
    rows = pairs * sub
    half = devices // 2
    upper = plus_ref[rows:, :].reshape(half, pairs, sub, LANES)
    for p in range(1, pairs):
        out_ref[:half, p] = upper[:, p].astype(jnp.bfloat16)
    before = plus_ref[: half * rows, :].reshape(half, pairs, sub, LANES)[:, 0]
    place = lax.broadcasted_iota(jnp.int32, before.shape, 1)
    out_ref[:half, 0] = jnp.where(place < sub // PAIR, before, upper[:, 0]).astype(jnp.bfloat16)
    for d in range(half):
        tile = minus_ref[(d + 1) * rows : (d + 2) * rows, :]
        out_ref[devices - 1 - d] = tile.astype(jnp.bfloat16).reshape(pairs, sub, LANES)


def head_kernel(
    samples_ref, taper_ref, table_ref, out_ref, first_ref,
    held_ref, fixed_ref, carry_ref, filtered0_ref, filtered1_ref, plus_ref, minus_ref,
    packed0_ref, packed1_ref, in_sems, table_sem, out_sems, first_sem,
):
    groups = held_ref.shape[0]
    rows = samples_ref.shape[0]
    filtered, packed = (filtered0_ref, filtered1_ref), (packed0_ref, packed1_ref)
    width = GROUP * NFFT

    def fetch(g):
        source = samples_ref.at[:, pl.ds(g * width, width)]
        return pltpu.make_async_copy(source, held_ref.at[g], in_sems.at[g])

    def send(g):
        return pltpu.make_async_copy(packed[g % 2], out_ref.at[:, :, g], out_sems.at[g % 2])

    table = pltpu.make_async_copy(table_ref, fixed_ref, table_sem)
    fetch(0).start()
    fetch(1).start()
    table.start()
    for g in range(2, groups):
        fetch(g).start()

    def past(t, part, chunk):
        lane = 2 * t * HALF + chunk * LANES
        return tuple(carry_ref[part, lane + s * HALF : lane + s * HALF + LANES] for s in range(2))

    def keep(t, part, chunk, value):
        lane = 2 * t * HALF + chunk * LANES
        for s in range(2):
            carry_ref[part, lane + s * HALF : lane + s * HALF + LANES] = value[s]

    def past_in(t, part, chunk):
        return frame_part(held_ref.at[0], part, GROUP - HALO + t, chunk)

    def past_own(t, part, chunk):
        return frame_part(held_ref.at[0], part, t, chunk)

    chunks = HALF // LANES
    fetch(0).wait()
    fetch(1).wait()
    for chunk in range(chunks):
        filter_chunk(held_ref.at[1], 0, GROUP, taper_ref, filtered[1], chunk, past_in, keep)
    table.wait()
    for g in range(1, groups):
        if g > 2:
            send(g - 2).wait()
        if g + 1 < groups:
            fetch(g + 1).wait()
        first = 0
        for i, count in enumerate(PARTS):
            transform_part(fixed_ref, filtered[g % 2], plus_ref, minus_ref, first, count)
            first += count
            share = chunks // len(PARTS)
            for chunk in range(i * share, (i + 1) * share):
                if g + 1 < groups:
                    filter_chunk(
                        held_ref.at[g + 1], 0, GROUP, taper_ref, filtered[(g + 1) % 2], chunk,
                        past, keep,
                    )
                else:
                    filter_chunk(
                        held_ref.at[0], HALO, GROUP - HALO, taper_ref, filtered[(g + 1) % 2], chunk,
                        past_own,
                    )
        pack(plus_ref, minus_ref, packed[g % 2])
        send(g).start()
    kept = pl.ds(HALO * rows, (GROUP - HALO) * rows)
    last = pltpu.make_async_copy(filtered[groups % 2].at[kept], first_ref, first_sem)
    last.start()
    last.wait()
    send(groups - 2).wait()
    send(groups - 1).wait()


def head(samples, taper, table, devices):
    rows, length = samples.shape
    groups = length // (GROUP * NFFT)
    pairs = CHANNELS // devices // PAIR
    width = GROUP * rows
    sub = 2 * PAIR * width // LANES
    spectra = (devices, pairs, groups, sub, LANES)
    packed = pltpu.VMEM((devices, pairs, sub, LANES), jnp.bfloat16)
    filtered = pltpu.VMEM((width, NFFT), jnp.bfloat16)
    turned = pltpu.VMEM((table.shape[0] * width // LANES, LANES), jnp.float32)
    return pl.pallas_call(
        head_kernel,
        in_specs=[
            pl.BlockSpec(memory_space=pltpu.HBM),
            pl.BlockSpec(memory_space=pltpu.VMEM),
            pl.BlockSpec(memory_space=pltpu.HBM),
        ],
        out_specs=[
            pl.BlockSpec(memory_space=pltpu.HBM),
            pl.BlockSpec(memory_space=pltpu.HBM),
        ],
        out_shape=[
            jax.ShapeDtypeStruct(spectra, jnp.bfloat16),
            jax.ShapeDtypeStruct(((GROUP - HALO) * rows, NFFT), jnp.bfloat16),
        ],
        scratch_shapes=[
            pltpu.VMEM((groups, rows, GROUP * NFFT), jnp.int32),
            pltpu.VMEM(table.shape, jnp.bfloat16),
            pltpu.VMEM((rows, HALO * NFFT), jnp.float32),
            filtered, filtered, turned, turned, packed, packed,
            pltpu.SemaphoreType.DMA((groups,)),
            pltpu.SemaphoreType.DMA,
            pltpu.SemaphoreType.DMA((2,)),
            pltpu.SemaphoreType.DMA,
        ],
        compiler_params=pltpu.CompilerParams(vmem_limit_bytes=60 * MIB),
        cost_estimate=pl.CostEstimate(
            flops=2 * table.shape[0] * NFFT * width * 3,
            bytes_accessed=2 * table.shape[0] * NFFT + 4 * rows * length,
            transcendentals=0,
        ),
        name="head",
    )(samples, taper, table)


def tail_kernel(
    samples_ref, halo_ref, first_ref, taper_ref, table_ref, _, out_ref,
    held_ref, halo_held_ref, fixed_ref, filtered_ref, plus_ref, minus_ref, packed_ref,
    in_sems, table_sems, out_sem,
):
    rows = samples_ref.shape[0]
    kept = pl.ds(HALO * rows, (GROUP - HALO) * rows)
    begin = samples_ref.at[:, pl.ds(0, HALO * NFFT)]
    copies = [
        pltpu.make_async_copy(begin, held_ref, in_sems.at[0]),
        pltpu.make_async_copy(halo_ref, halo_held_ref, in_sems.at[1]),
        pltpu.make_async_copy(first_ref, filtered_ref.at[kept], in_sems.at[2]),
    ]
    tables = []
    first = 0
    for i, count in enumerate(PARTS):
        part = pl.ds(first, count)
        tables.append(
            pltpu.make_async_copy(table_ref.at[part], fixed_ref.at[part], table_sems.at[i])
        )
        first += count
    for copy in copies + tables:
        copy.start()

    def past(t, part, chunk):
        return frame_part(halo_held_ref, part, t, chunk)

    copies[0].wait()
    copies[1].wait()
    for chunk in range(HALF // LANES):
        filter_chunk(held_ref, 0, HALO, taper_ref, filtered_ref, chunk, past)
    copies[2].wait()
    first = 0
    for i, count in enumerate(PARTS):
        tables[i].wait()
        transform_part(fixed_ref, filtered_ref, plus_ref, minus_ref, first, count)
        first += count
    pack(plus_ref, minus_ref, packed_ref)
    send = pltpu.make_async_copy(packed_ref, out_ref.at[:, :, 0], out_sem)
    send.start()
    send.wait()


def tail(samples, halo, first, taper, table, spectra):
    rows = samples.shape[0]
    width = GROUP * rows
    devices, pairs, groups, sub, _ = spectra.shape
    turned = pltpu.VMEM((table.shape[0] * width // LANES, LANES), jnp.float32)
    return pl.pallas_call(
        tail_kernel,
        in_specs=[
            pl.BlockSpec(memory_space=pltpu.HBM),
            pl.BlockSpec(memory_space=pl.ANY),
            pl.BlockSpec(memory_space=pltpu.HBM),
            pl.BlockSpec(memory_space=pltpu.VMEM),
            pl.BlockSpec(memory_space=pltpu.HBM),
            pl.BlockSpec(memory_space=pltpu.HBM),
        ],
        out_specs=pl.BlockSpec(memory_space=pltpu.HBM),
        out_shape=jax.ShapeDtypeStruct(spectra.shape, spectra.dtype),
        scratch_shapes=[
            pltpu.VMEM((rows, HALO * NFFT), jnp.int32),
            pltpu.VMEM((rows, HALO * NFFT), jnp.bfloat16),
            pltpu.VMEM(table.shape, jnp.bfloat16),
            pltpu.VMEM((width, NFFT), jnp.bfloat16),
            turned, turned,
            pltpu.VMEM((devices, pairs, sub, LANES), jnp.bfloat16),
            pltpu.SemaphoreType.DMA((3,)),
            pltpu.SemaphoreType.DMA((len(PARTS),)),
            pltpu.SemaphoreType.DMA,
        ],
        input_output_aliases={5: 0},
        compiler_params=pltpu.CompilerParams(vmem_limit_bytes=60 * MIB),
        cost_estimate=pl.CostEstimate(
            flops=2 * table.shape[0] * NFFT * width,
            bytes_accessed=2 * table.shape[0] * NFFT,
            transcendentals=0,
        ),
        name="tail",
    )(samples, halo, first, taper, table, spectra)


def lane_turn(parts, block):
    lane = lax.broadcasted_iota(jnp.int32, parts[0].shape, 1)
    for step in (2, 1):
        upper = (lane // (block * step)) % 2 == 1
        turned = list(parts)
        for p in range(4):
            if p & step:
                continue
            low, high = parts[p], parts[p + step]
            turned[p] = jnp.where(upper, pltpu.roll(high, step * block, 1), low)
            turned[p + step] = jnp.where(upper, high, pltpu.roll(low, LANES - step * block, 1))
        parts = turned
    return parts


def spread(x, wide_ref):
    wide_ref[...] = x.astype(jnp.float32).reshape(wide_ref.shape)


def arrange(wide_ref, turned_ref, channel, feeds):
    each = wide_ref.shape[0] // feeds
    high = each // 8
    block = turned_ref.shape[1] // feeds
    inner = LANES // block
    half = turned_ref.shape[0] // 2
    for first in range(0, feeds, inner):
        for r in range(2):
            parts = []
            for f in range(first, first + inner):
                start = f * each + 4 * channel + 2 * r
                both = [wide_ref[pl.ds(start + j, high, stride=8), :] for j in range(2)]
                parts.append(jnp.concatenate(both, axis=0).astype(jnp.bfloat16))
            for k, side in enumerate(lane_turn(parts, block)):
                row = r * half + 2 * k * high
                turned_ref[row : row + 2 * high, first * block : (first + inner) * block] = side


def product(a, b):
    return lax.dot_general(a, b, (((1,), (1,)), ((), ())), preferred_element_type=jnp.float32)


def order(turned_ref, place_ref, z_ref):
    inputs = place_ref.shape[0]
    frames = turned_ref.shape[0] // 2
    z = product(place_ref[...], turned_ref[...])
    z_ref[:inputs] = z.astype(jnp.bfloat16)
    z_ref[inputs:, :frames] = z[:, frames:].astype(jnp.bfloat16)
    z_ref[inputs:, frames:] = (-z[:, :frames]).astype(jnp.bfloat16)


def correlate(z_ref, out_ref, norm):
    inputs = z_ref.shape[1]
    value = norm * product(z_ref[...], z_ref[:inputs])
    out_ref[0] = value[:inputs]
    out_ref[1] = value[inputs:]


def gram_kernel(
    feeds, norm, upper_ref, x_ref, place_ref, out_ref, held_ref, wide_ref, turned0_ref, turned1_ref,
    z0_ref, z1_ref, done0_ref, done1_ref, in_sems, out_sems,
):
    turned, z, done = (turned0_ref, turned1_ref), (z0_ref, z1_ref), (done0_ref, done1_ref)
    pairs = x_ref.shape[1]

    def fetch(pair):
        return pltpu.make_async_copy(x_ref.at[:, pair], held_ref.at[pair], in_sems.at[pair])

    def send(pair, parity):
        low, high = (pair, PAIR * pairs - pair)
        first = upper_ref[0] == parity
        local = jnp.where(pair == 0, parity * pairs, jnp.where(first, low, high))
        return pltpu.make_async_copy(done[parity], out_ref.at[local], out_sems.at[parity])

    def phase(pair, parity, third=True, second=True, first=True, wait=True):
        if first and parity == 0:
            fetch(pair).wait()
        if third:
            if wait:
                send(pair - 2, parity).wait()
            correlate(z[parity], done[parity], norm)
        if second:
            order(turned[1 - parity], place_ref, z[1 - parity])
        if first:
            if parity == 0:
                spread(held_ref[pair], wide_ref)
            arrange(wide_ref, turned[parity], parity, feeds)
        if third:
            send(pair - 1, parity).start()

    for pair in range(pairs):
        fetch(pair).start()
    phase(0, 0, third=False, second=False)
    phase(0, 1, third=False)
    phase(1, 0, wait=False)
    phase(1, 1, wait=False)

    def body(pair, _):
        phase(pair, 0)
        phase(pair, 1)
        return 0

    lax.fori_loop(2, pairs, body, 0)
    phase(pairs, 0, first=False)
    phase(pairs, 1, second=False, first=False)
    for parity in range(PAIR):
        send(pairs - 1, parity).wait()


def grams(upper, incoming, place, feeds):
    devices, pairs, groups, sub, _ = incoming.shape
    channels = PAIR * pairs
    inputs = place.shape[0]
    frames = devices * groups * sub * LANES // (2 * PAIR * inputs)
    return pl.pallas_call(
        functools.partial(gram_kernel, feeds, 1.0 / math.sqrt(frames)),
        in_specs=[
            pl.BlockSpec(memory_space=pltpu.SMEM),
            pl.BlockSpec(memory_space=pl.ANY),
            pl.BlockSpec(memory_space=pltpu.VMEM),
        ],
        out_specs=pl.BlockSpec(memory_space=pl.ANY),
        out_shape=jax.ShapeDtypeStruct((channels, 2, inputs, inputs), jnp.float32),
        scratch_shapes=[
            pltpu.VMEM((pairs, devices, groups, sub, LANES), jnp.bfloat16),
            pltpu.VMEM((devices * groups * sub, LANES), jnp.float32),
            pltpu.VMEM((2 * frames, inputs), jnp.bfloat16),
            pltpu.VMEM((2 * frames, inputs), jnp.bfloat16),
            pltpu.VMEM((2 * inputs, 2 * frames), jnp.bfloat16),
            pltpu.VMEM((2 * inputs, 2 * frames), jnp.bfloat16),
            pltpu.VMEM((2, inputs, inputs), jnp.float32),
            pltpu.VMEM((2, inputs, inputs), jnp.float32),
            pltpu.SemaphoreType.DMA((pairs,)),
            pltpu.SemaphoreType.DMA((PAIR,)),
        ],
        compiler_params=pltpu.CompilerParams(vmem_limit_bytes=60 * MIB),
        cost_estimate=pl.CostEstimate(
            flops=channels * 12 * inputs * inputs * frames,
            bytes_accessed=channels * (8 * inputs * inputs + 4 * inputs * frames),
            transcendentals=0,
        ),
        name="gram",
    )(upper, incoming, place)


def per_device(samples, input_map):
    feeds = lax.axis_size("feed")
    times = lax.axis_size("tm")
    devices = feeds * times
    inputs = input_map.shape[0]
    taper = jnp.asarray(taper_table())
    table = jnp.asarray(transform_table(devices))
    last = samples[:, samples.shape[1] - HALO * NFFT :].astype(jnp.bfloat16)
    halo = lax.ppermute(last, "tm", [(t, t + 1) for t in range(times - 1)])
    place = (input_map[:, None] == jnp.arange(inputs)[None, :]).astype(jnp.bfloat16)
    device = lax.axis_index("feed") * times + lax.axis_index("tm")
    upper = (2 * device // devices).astype(jnp.int32).reshape(1)
    spectra, first = head(samples, taper, table, devices)
    outgoing = tail(samples, halo, first, taper, table, spectra)
    incoming = lax.all_to_all(outgoing, ("feed", "tm"), split_axis=0, concat_axis=0, tiled=True)
    return grams(upper, incoming, place, feeds)


def solution(mesh):
    in_specs = (P("feed", "tm"), P())
    out_specs = P(("feed", "tm"), None, None, None)
    return jax.shard_map(
        per_device, mesh=mesh, in_specs=in_specs, out_specs=out_specs, check_vma=False
    )
```

time: 107 us -> 101 us (0.944)
  Pallas kernels: 35.8 us -> 29.6 us
    pallas_call x2, Pallas kernels: 22.7 us -> 16.4 us  [the longest x1 10.9 us: head(): pl.pallas_call(head_kernel, in_specs=[pl.BlockSpec(memory_space=pltpu.HBM...]
  transfers between devices with their start and end apart: 2 -> 2, of which waited for: 1 -> 1; matrix products, arithmetic and copies ran while one was open for 1% -> 1% of each run, Pallas kernels for 15% -> 11%
where the time goes in v3:
time: 101 us
  waiting for transfers between devices  52.7 us (52%)
  Pallas kernels  29.6 us (29%)
  starting transfers between devices  15.1 us (15%)
  other arithmetic  2.14 us (2%)
    all_to_all x1, waiting for transfers between devices, per_device(): lax.all_to_all(outgoing, ('feed', 'tm'), split_axis=0, concat_axis=0, til...  52.7 us
    pallas_call x1, Pallas kernels, grams(): pl.pallas_call(functools.partial(gram_kernel, feeds, 1.0 / math.sqrt(fram...  13.2 us
    all_to_all x1, starting transfers between devices, per_device(): lax.all_to_all(outgoing, ('feed', 'tm'), split_axis=0, concat_axis=0, til...  11.1 us
    pallas_call x1, Pallas kernels, head(): pl.pallas_call(head_kernel, in_specs=[pl.BlockSpec(memory_space=pltpu.HBM...  10.9 us
    pallas_call x1, Pallas kernels, tail(): pl.pallas_call(tail_kernel, in_specs=[pl.BlockSpec(memory_space=pltpu.HBM...  5.5 us
    ppermute x1, starting transfers between devices, per_device(): halo = lax.ppermute(last, 'tm', [(t, t + 1) for t in range(times - 1)])  3.97 us
  transfers between devices with their start and end apart: 2, of which 1 were waited for; matrix products, arithmetic and copies ran while one was open for 1% of the time, Pallas kernels for 11%

profile of v3, /device:TPU:1, one launch (start us, length us, event | category | flops | bytes accessed | tf_op | source)
XLA Modules:
  0.0 100.5 jit_solution(9798909015454266846)
XLA Ops:
  0.0 1.2 %slice_convert_fusion = bf16[32,6144]{1,0:T(8,128)(2,1)S(1)} fusion(s32[32,65536]{1,0:T(8,128)} %samples_ref.3), kind=kLoop, calls=%fused_computation.2 | loop fusion | flops 196608 | bytes 1179648 | tf_op jit(solution)/shard_map/convert
  1.2 4.0 %collective-permute-start = (bf16[32,6144]{1,0:T(8,128)(2,1)S(1)}, bf16[32,6144]{1,0:T(8,128)(2,1)S(1)}, u32[]{:S(2)}, u32[]{:S(2)}) collective-permute-start(bf16[32,6144]{1,0:T(8,128)(2,1)S(1)} %slice_convert_fusion), channel_id=1, source_target_pairs={{0,1},{1,2},{2,3},{3,4},{4,5},{5,6},{6,7},{8,9},{9,10},{10,11},{11... | collective-permute-start | bytes 1179656 | tf_op jit(solution)/shard_map/ppermute | solution.py:481
  5.2 10.9 %head.1 = (bf16[128,4,4,8,128]{4,3,2,1,0:T(8,128)(2,1)}, bf16[160,2048]{1,0:T(8,128)(2,1)}) custom-call(s32[32,65536]{1,0:T(8,128)} %samples_ref.3, f32[4,2048]{1,0:T(4,128)} %constant.33.clone.taper_ref, bf16[1040,2048]{1,0:T(8,128)(2,1)} %constant.34.clone.table_ref), custom_call_target="tpu_custom_call" | custom-call | flops 3271557120 | bytes 12648448 | tf_op jit(solution)/shard_map/head/pallas_call | solution.py:212
  16.1 0.0 collective-permute-done.halo_ref
  16.1 0.0 copy-start
  16.1 0.7 copy-done
  16.9 5.5 %tail.1 = bf16[128,4,4,8,128]{4,3,2,1,0:T(8,128)(2,1)} custom-call(s32[32,65536]{1,0:T(8,128)} %samples_ref.3, bf16[32,6144]{1,0:T(8,128)(2,1)} %copy-done, bf16[160,2048]{1,0:T(8,128)(2,1)} %get-tuple-element.7.first_ref, f32[4,2048]{1,0:T(4,128)} %constant.33.clone.taper_ref, ...), custom_call_target="tpu_custom_call", output_to_operand_aliasing={{}: (5, {})} | custom-call | flops 1090519040 | bytes 4259840 | tf_op jit(solution)/shard_map/tail/pallas_call | solution.py:295
  22.4 0.0 copy-start.1
  22.4 11.1 %all-to-all-start = ((bf16[128,4,4,8,128]{4,3,2,1,0:T(8,128)(2,1)}), bf16[128,4,4,8,128]{4,3,2,1,0:T(8,128)(2,1)}, u32[]{:S(2)}, u32[]{:S(2)}) async-start(bf16[128,4,4,8,128]{4,3,2,1,0:T(8,128)(2,1)} %tail.1), calls=%async_computation | async-start | bytes 8388608 | tf_op jit(solution)/shard_map/all_to_all | solution.py:487
  33.5 0.0 copy-done.1
  33.5 1.0 fusion.place_ref
  34.5 52.7 %all-to-all-done.x_ref = bf16[128,4,4,8,128]{4,3,2,1,0:T(8,128)(2,1)} async-done(((bf16[128,4,4,8,128]{4,3,2,1,0:T(8,128)(2,1)}), bf16[128,4,4,8,128]{4,3,2,1,0:T(8,128)(2,1)}, u32[]{:S(2)}, u32[]{:S(2)}) %all-to-all-start) | async-done | bytes 4194336 | tf_op jit(solution)/shard_map/all_to_all | solution.py:487
  87.2 13.2 %gram.1 = f32[8,2,512,512]{3,2,1,0:T(8,128)} custom-call(s32[1]{0:T(128)} %bitcast.upper_ref, bf16[128,4,4,8,128]{4,3,2,1,0:T(8,128)(2,1)} %all-to-all-done.x_ref, bf16[512,512]{1,0:T(8,128)(2,1)} %fusion.place_ref), custom_call_target="tpu_custom_call" | custom-call | flops 6442450944 | bytes 20971520 | tf_op jit(solution)/shard_map/gram/pallas_call | solution.py:442
Async XLA Ops:
  1.2 14.9 %collective-permute-start = (bf16[32,6144]{1,0:T(8,128)(2,1)S(1)}, bf16[32,6144]{1,0:T(8,128)(2,1)S(1)}, u32[]{:S(2)}, u32[]{:S(2)}) collective-permute-start(bf16[32,6144]{1,0:T(8,128)(2,1)S(1)} %slice_convert_fusion), channel_id=1, source_target_pairs={{0,1},{1,2},{2,3},{3,4},{4,5},{5,6},{6,7},{8,9},{9,10},{10,11},{11... | collective-permute-start | bytes 1179656 | tf_op jit(solution)/shard_map/ppermute | solution.py:481
  16.1 0.7 copy-start
  22.4 11.2 %copy-start.1 = (s32[512]{0:T(512)S(1)}, s32[512]{0:T(512)}, u32[]{:S(2)}) copy-start(s32[512]{0:T(512)} %param.5) | copy-start | bytes 6148
  22.4 64.8 %all-to-all-start = ((bf16[128,4,4,8,128]{4,3,2,1,0:T(8,128)(2,1)}), bf16[128,4,4,8,128]{4,3,2,1,0:T(8,128)(2,1)}, u32[]{:S(2)}, u32[]{:S(2)}) async-start(bf16[128,4,4,8,128]{4,3,2,1,0:T(8,128)(2,1)} %tail.1), calls=%async_computation | async-start | bytes 8388608 | tf_op jit(solution)/shard_map/all_to_all | solution.py:487

commit v4 on v3

--- a/solution.py
+++ b/solution.py
@@ -74,7 +74,7 @@
     return separate(*both)
 
 
-def filter_chunk(ref, first, frames, taper_ref, out_ref, chunk, past, keep=None):
+def filter_chunk(ref, frames, taper_ref, out_ref, place, chunk, past, keep=None):
     rows = ref.shape[0]
     lanes = [slice(side * HALF + chunk * LANES, side * HALF + (chunk + 1) * LANES) for side in range(2)]
     taper = [[taper_ref[tap : tap + 1, lane] for tap in range(TAPS)] for lane in lanes]
@@ -82,13 +82,13 @@
         part = slice(row, row + 16)
         x = [past(t, part, chunk) for t in range(HALO)]
         for k in range(frames):
-            x.append(frame_part(ref, part, first + k, chunk))
+            x.append(frame_part(ref, part, k, chunk))
             for side in range(2):
                 value = taper[side][0] * x[k][side]
                 for tap in range(1, TAPS):
                     value = value + taper[side][tap] * x[k + tap][side]
-                place = (first + k) % GROUP * rows + row
-                out_ref[place : place + 16, lanes[side]] = value.astype(jnp.bfloat16)
+                start = (place + k) * rows + row
+                out_ref[start : start + 16, lanes[side]] = value.astype(jnp.bfloat16)
         if keep is not None:
             for t in range(HALO):
                 keep(t, part, chunk, x[frames + t])
@@ -108,7 +108,7 @@
         minus_ref[pl.ds(first * total + j, count, stride=total), :] = sign * (e - o)
 
 
-def pack(plus_ref, minus_ref, out_ref):
+def pack_lower(plus_ref, out_ref):
     devices, pairs, sub, _ = out_ref.shape
     rows = pairs * sub
     half = devices // 2
@@ -118,34 +118,48 @@
     before = plus_ref[: half * rows, :].reshape(half, pairs, sub, LANES)[:, 0]
     place = lax.broadcasted_iota(jnp.int32, before.shape, 1)
     out_ref[:half, 0] = jnp.where(place < sub // PAIR, before, upper[:, 0]).astype(jnp.bfloat16)
-    for d in range(half):
+
+
+def pack_upper(minus_ref, out_ref):
+    devices, pairs, sub, _ = out_ref.shape
+    rows = pairs * sub
+    for d in range(devices // 2):
         tile = minus_ref[(d + 1) * rows : (d + 2) * rows, :]
         out_ref[devices - 1 - d] = tile.astype(jnp.bfloat16).reshape(pairs, sub, LANES)
 
 
 def head_kernel(
-    samples_ref, taper_ref, table_ref, out_ref, first_ref,
-    held_ref, fixed_ref, carry_ref, filtered0_ref, filtered1_ref, plus_ref, minus_ref,
-    packed0_ref, packed1_ref, in_sems, table_sem, out_sems, first_sem,
+    samples_ref, curve_ref, table_ref, out_ref, first_ref, begin_ref, taper_ref, fixed_ref,
+    rest_ref, held_ref, carry_ref, filtered0_ref, filtered1_ref, plus0_ref, plus1_ref,
+    minus0_ref, minus1_ref, packed0_ref, packed1_ref, in_sems, out_sems,
 ):
-    groups = held_ref.shape[0]
-    rows = samples_ref.shape[0]
+    groups = held_ref.shape[0] + 1
     filtered, packed = (filtered0_ref, filtered1_ref), (packed0_ref, packed1_ref)
+    plus, minus = (plus0_ref, plus1_ref), (minus0_ref, minus1_ref)
     width = GROUP * NFFT
 
     def fetch(g):
         source = samples_ref.at[:, pl.ds(g * width, width)]
-        return pltpu.make_async_copy(source, held_ref.at[g], in_sems.at[g])
+        return pltpu.make_async_copy(source, held_ref.at[g - 1], in_sems.at[g])
 
     def send(g):
         return pltpu.make_async_copy(packed[g % 2], out_ref.at[:, :, g], out_sems.at[g % 2])
 
-    table = pltpu.make_async_copy(table_ref, fixed_ref, table_sem)
-    fetch(0).start()
+    begin = pltpu.make_async_copy(
+        samples_ref.at[:, pl.ds(0, HALO * NFFT)], begin_ref, in_sems.at[0]
+    )
+    rest = pltpu.make_async_copy(
+        samples_ref.at[:, pl.ds(HALO * NFFT, (GROUP - HALO) * NFFT)], rest_ref, in_sems.at[groups]
+    )
+    table = pltpu.make_async_copy(table_ref, fixed_ref, in_sems.at[groups + 1])
+    taper = pltpu.make_async_copy(curve_ref, taper_ref, in_sems.at[groups + 2])
+    taper.start()
+    rest.start()
     fetch(1).start()
     table.start()
     for g in range(2, groups):
         fetch(g).start()
+    begin.start()
 
     def past(t, part, chunk):
         lane = 2 * t * HALF + chunk * LANES
@@ -157,46 +171,62 @@
             carry_ref[part, lane + s * HALF : lane + s * HALF + LANES] = value[s]
 
     def past_in(t, part, chunk):
-        return frame_part(held_ref.at[0], part, GROUP - HALO + t, chunk)
+        return frame_part(rest_ref, part, GROUP - 2 * HALO + t, chunk)
 
     def past_own(t, part, chunk):
-        return frame_part(held_ref.at[0], part, t, chunk)
+        return frame_part(begin_ref, part, t, chunk)
 
     chunks = HALF // LANES
-    fetch(0).wait()
+    taper.wait()
+    rest.wait()
     fetch(1).wait()
     for chunk in range(chunks):
-        filter_chunk(held_ref.at[1], 0, GROUP, taper_ref, filtered[1], chunk, past_in, keep)
+        filter_chunk(held_ref.at[0], GROUP, taper_ref, filtered[1], 0, chunk, past_in, keep)
     table.wait()
     for g in range(1, groups):
-        if g > 2:
-            send(g - 2).wait()
+        now = g % 2
         if g + 1 < groups:
             fetch(g + 1).wait()
+        else:
+            begin.wait()
+        if g > 3:
+            send(g - 3).wait()
         first = 0
         for i, count in enumerate(PARTS):
-            transform_part(fixed_ref, filtered[g % 2], plus_ref, minus_ref, first, count)
+            transform_part(fixed_ref, filtered[now], plus[now], minus[now], first, count)
             first += count
+            if g > 1:
+                if i == 0:
+                    pack_lower(plus[1 - now], packed[1 - now])
+                if i == len(PARTS) - 1:
+                    pack_upper(minus[1 - now], packed[1 - now])
             share = chunks // len(PARTS)
             for chunk in range(i * share, (i + 1) * share):
                 if g + 1 < groups:
                     filter_chunk(
-                        held_ref.at[g + 1], 0, GROUP, taper_ref, filtered[(g + 1) % 2], chunk,
-                        past, keep,
+                        held_ref.at[g], GROUP, taper_ref, filtered[1 - now], 0, chunk, past, keep
                     )
                 else:
                     filter_chunk(
-                        held_ref.at[0], HALO, GROUP - HALO, taper_ref, filtered[(g + 1) % 2], chunk,
-                        past_own,
+                        rest_ref, GROUP - HALO, taper_ref, first_ref, HALO, chunk, past_own
                     )
-        pack(plus_ref, minus_ref, packed[g % 2])
-        send(g).start()
-    kept = pl.ds(HALO * rows, (GROUP - HALO) * rows)
-    last = pltpu.make_async_copy(filtered[groups % 2].at[kept], first_ref, first_sem)
-    last.start()
-    last.wait()
+        if g > 1:
+            send(g - 1).start()
+    last = (groups - 1) % 2
+    send(groups - 3).wait()
+    pack_lower(plus[last], packed[last])
+    pack_upper(minus[last], packed[last])
+    send(groups - 1).start()
     send(groups - 2).wait()
     send(groups - 1).wait()
+
+
+def in_hbm(*values):
+    return tuple(pltpu.with_memory_space_constraint(value, pltpu.HBM) for value in values)
+
+
+def in_vmem(*values):
+    return tuple(pltpu.with_memory_space_constraint(value, pltpu.VMEM) for value in values)
 
 
 def head(samples, taper, table, devices):
@@ -213,117 +243,92 @@
         head_kernel,
         in_specs=[
             pl.BlockSpec(memory_space=pltpu.HBM),
-            pl.BlockSpec(memory_space=pltpu.VMEM),
-            pl.BlockSpec(memory_space=pltpu.HBM),
-        ],
-        out_specs=[
             pl.BlockSpec(memory_space=pltpu.HBM),
             pl.BlockSpec(memory_space=pltpu.HBM),
         ],
+        out_specs=[pl.BlockSpec(memory_space=pltpu.HBM)]
+        + [pl.BlockSpec(memory_space=pltpu.VMEM)] * 4,
         out_shape=[
-            jax.ShapeDtypeStruct(spectra, jnp.bfloat16),
-            jax.ShapeDtypeStruct(((GROUP - HALO) * rows, NFFT), jnp.bfloat16),
+            pltpu.HBM(spectra, jnp.bfloat16),
+            pltpu.VMEM((width, NFFT), jnp.bfloat16),
+            pltpu.VMEM((rows, HALO * NFFT), jnp.int32),
+            pltpu.VMEM(taper.shape, jnp.float32),
+            pltpu.VMEM(table.shape, jnp.bfloat16),
         ],
         scratch_shapes=[
-            pltpu.VMEM((groups, rows, GROUP * NFFT), jnp.int32),
-            pltpu.VMEM(table.shape, jnp.bfloat16),
+            pltpu.VMEM((rows, (GROUP - HALO) * NFFT), jnp.int32),
+            pltpu.VMEM((groups - 1, rows, GROUP * NFFT), jnp.int32),
             pltpu.VMEM((rows, HALO * NFFT), jnp.float32),
-            filtered, filtered, turned, turned, packed, packed,
-            pltpu.SemaphoreType.DMA((groups,)),
-            pltpu.SemaphoreType.DMA,
+            filtered, filtered, turned, turned, turned, turned, packed, packed,
+            pltpu.SemaphoreType.DMA((groups + 3,)),
             pltpu.SemaphoreType.DMA((2,)),
-            pltpu.SemaphoreType.DMA,
         ],
-        compiler_params=pltpu.CompilerParams(vmem_limit_bytes=60 * MIB),
+        compiler_params=pltpu.CompilerParams(vmem_limit_bytes=40 * MIB),
         cost_estimate=pl.CostEstimate(
             flops=2 * table.shape[0] * NFFT * width * 3,
             bytes_accessed=2 * table.shape[0] * NFFT + 4 * rows * length,
             transcendentals=0,
         ),
         name="head",
-    )(samples, taper, table)
+    )(*in_hbm(samples, taper, table))
 
 
 def tail_kernel(
-    samples_ref, halo_ref, first_ref, taper_ref, table_ref, _, out_ref,
-    held_ref, halo_held_ref, fixed_ref, filtered_ref, plus_ref, minus_ref, packed_ref,
-    in_sems, table_sems, out_sem,
+    begin_ref, halo_ref, first_ref, taper_ref, fixed_ref, _, out_ref,
+    filtered_ref, plus_ref, minus_ref, packed_ref, out_sems,
 ):
-    rows = samples_ref.shape[0]
-    kept = pl.ds(HALO * rows, (GROUP - HALO) * rows)
-    begin = samples_ref.at[:, pl.ds(0, HALO * NFFT)]
-    copies = [
-        pltpu.make_async_copy(begin, held_ref, in_sems.at[0]),
-        pltpu.make_async_copy(halo_ref, halo_held_ref, in_sems.at[1]),
-        pltpu.make_async_copy(first_ref, filtered_ref.at[kept], in_sems.at[2]),
-    ]
-    tables = []
+    rows = begin_ref.shape[0]
+    kept = HALO * rows
+    half = packed_ref.shape[0] // 2
+
+    def past(t, part, chunk):
+        return frame_part(halo_ref, part, t, chunk)
+
+    def send(side):
+        part = pl.ds(side * half, half)
+        return pltpu.make_async_copy(packed_ref.at[part], out_ref.at[part, :, 0], out_sems.at[side])
+
+    filtered_ref[kept:, :] = first_ref[kept:, :]
+    for chunk in range(HALF // LANES):
+        filter_chunk(begin_ref, HALO, taper_ref, filtered_ref, 0, chunk, past)
     first = 0
-    for i, count in enumerate(PARTS):
-        part = pl.ds(first, count)
-        tables.append(
-            pltpu.make_async_copy(table_ref.at[part], fixed_ref.at[part], table_sems.at[i])
-        )
-        first += count
-    for copy in copies + tables:
-        copy.start()
-
-    def past(t, part, chunk):
-        return frame_part(halo_held_ref, part, t, chunk)
-
-    copies[0].wait()
-    copies[1].wait()
-    for chunk in range(HALF // LANES):
-        filter_chunk(held_ref, 0, HALO, taper_ref, filtered_ref, chunk, past)
-    copies[2].wait()
-    first = 0
-    for i, count in enumerate(PARTS):
-        tables[i].wait()
+    for count in PARTS:
         transform_part(fixed_ref, filtered_ref, plus_ref, minus_ref, first, count)
         first += count
-    pack(plus_ref, minus_ref, packed_ref)
-    send = pltpu.make_async_copy(packed_ref, out_ref.at[:, :, 0], out_sem)
-    send.start()
-    send.wait()
-
-
-def tail(samples, halo, first, taper, table, spectra):
-    rows = samples.shape[0]
+    pack_lower(plus_ref, packed_ref)
+    send(0).start()
+    pack_upper(minus_ref, packed_ref)
+    send(1).start()
+    send(0).wait()
+    send(1).wait()
+
+
+def tail(begin, halo, first, taper, fixed, spectra):
+    rows = begin.shape[0]
     width = GROUP * rows
-    devices, pairs, groups, sub, _ = spectra.shape
-    turned = pltpu.VMEM((table.shape[0] * width // LANES, LANES), jnp.float32)
+    devices, pairs, _, sub, _ = spectra.shape
+    turned = pltpu.VMEM((fixed.shape[0] * width // LANES, LANES), jnp.float32)
     return pl.pallas_call(
         tail_kernel,
-        in_specs=[
-            pl.BlockSpec(memory_space=pltpu.HBM),
-            pl.BlockSpec(memory_space=pl.ANY),
-            pl.BlockSpec(memory_space=pltpu.HBM),
-            pl.BlockSpec(memory_space=pltpu.VMEM),
-            pl.BlockSpec(memory_space=pltpu.HBM),
-            pl.BlockSpec(memory_space=pltpu.HBM),
-        ],
+        in_specs=[pl.BlockSpec(memory_space=pltpu.VMEM)] * 5
+        + [pl.BlockSpec(memory_space=pltpu.HBM)],
         out_specs=pl.BlockSpec(memory_space=pltpu.HBM),
-        out_shape=jax.ShapeDtypeStruct(spectra.shape, spectra.dtype),
+        out_shape=pltpu.HBM(spectra.shape, spectra.dtype),
         scratch_shapes=[
-            pltpu.VMEM((rows, HALO * NFFT), jnp.int32),
-            pltpu.VMEM((rows, HALO * NFFT), jnp.bfloat16),
-            pltpu.VMEM(table.shape, jnp.bfloat16),
             pltpu.VMEM((width, NFFT), jnp.bfloat16),
             turned, turned,
             pltpu.VMEM((devices, pairs, sub, LANES), jnp.bfloat16),
-            pltpu.SemaphoreType.DMA((3,)),
-            pltpu.SemaphoreType.DMA((len(PARTS),)),
-            pltpu.SemaphoreType.DMA,
+            pltpu.SemaphoreType.DMA((2,)),
         ],
         input_output_aliases={5: 0},
-        compiler_params=pltpu.CompilerParams(vmem_limit_bytes=60 * MIB),
+        compiler_params=pltpu.CompilerParams(vmem_limit_bytes=32 * MIB),
         cost_estimate=pl.CostEstimate(
-            flops=2 * table.shape[0] * NFFT * width,
-            bytes_accessed=2 * table.shape[0] * NFFT,
+            flops=2 * fixed.shape[0] * NFFT * width,
+            bytes_accessed=2 * fixed.shape[0] * NFFT,
             transcendentals=0,
         ),
         name="tail",
-    )(samples, halo, first, taper, table, spectra)
+    )(*in_vmem(begin, halo, first, taper, fixed), *in_hbm(spectra))
 
 
 def lane_turn(parts, block):
@@ -399,9 +404,12 @@
         local = jnp.where(pair == 0, parity * pairs, jnp.where(first, low, high))
         return pltpu.make_async_copy(done[parity], out_ref.at[local], out_sems.at[parity])
 
-    def phase(pair, parity, third=True, second=True, first=True, wait=True):
+    def phase(pair, parity, third=True, second=True, first=True, wait=True, wait_more=True):
         if first and parity == 0:
             fetch(pair).wait()
+            if not wait_more:
+                for later in range(1, pairs):
+                    fetch(later).start()
         if third:
             if wait:
                 send(pair - 2, parity).wait()
@@ -415,9 +423,8 @@
         if third:
             send(pair - 1, parity).start()
 
-    for pair in range(pairs):
-        fetch(pair).start()
-    phase(0, 0, third=False, second=False)
+    fetch(0).start()
+    phase(0, 0, third=False, second=False, wait_more=False)
     phase(0, 1, third=False)
     phase(1, 0, wait=False)
     phase(1, 1, wait=False)
@@ -460,14 +467,14 @@
             pltpu.SemaphoreType.DMA((pairs,)),
             pltpu.SemaphoreType.DMA((PAIR,)),
         ],
-        compiler_params=pltpu.CompilerParams(vmem_limit_bytes=60 * MIB),
+        compiler_params=pltpu.CompilerParams(vmem_limit_bytes=40 * MIB),
         cost_estimate=pl.CostEstimate(
             flops=channels * 12 * inputs * inputs * frames,
             bytes_accessed=channels * (8 * inputs * inputs + 4 * inputs * frames),
             transcendentals=0,
         ),
         name="gram",
-    )(upper, incoming, place)
+    )(upper, *in_hbm(incoming), place)
 
 
 def per_device(samples, input_map):
@@ -482,8 +489,9 @@
     place = (input_map[:, None] == jnp.arange(inputs)[None, :]).astype(jnp.bfloat16)
     device = lax.axis_index("feed") * times + lax.axis_index("tm")
     upper = (2 * device // devices).astype(jnp.int32).reshape(1)
-    spectra, first = head(samples, taper, table, devices)
-    outgoing = tail(samples, halo, first, taper, table, spectra)
+    spectra, *held = head(samples, taper, table, devices)
+    first, begin, curve, fixed = held
+    outgoing = tail(begin, halo, first, curve, fixed, spectra)
     incoming = lax.all_to_all(outgoing, ("feed", "tm"), split_axis=0, concat_axis=0, tiled=True)
     return grams(upper, incoming, place, feeds)
 

time: 101 us -> 95.2 us (0.943)
  Pallas kernels: 29.6 us -> 24.7 us
    pallas_call x1, Pallas kernels: 5.5 us -> 2.77 us  [tail(): pl.pallas_call(tail_kernel, in_specs=[pl.BlockSpec(memory_space=pltpu.VME...]
    pallas_call x1, Pallas kernels: 10.9 us -> 9.77 us  [head(): pl.pallas_call(head_kernel, in_specs=[pl.BlockSpec(memory_space=pltpu.HBM...]
    pallas_call x1, Pallas kernels: 13.2 us -> 12.1 us  [grams(): pl.pallas_call(functools.partial(gram_kernel, feeds, 1.0 / math.sqrt(fram...]
  transfers between devices with their start and end apart: 2 -> 2, of which waited for: 1 -> 1; matrix products, arithmetic and copies ran while one was open for 1% -> 0% of each run, Pallas kernels for 11% -> 10%
where the time goes in v4:
time: 95.2 us; the launch traced here: 94.9 us
  waiting for transfers between devices  53.5 us (56%)
  Pallas kernels  24.7 us (26%)
  starting transfers between devices  15.1 us (16%)
  other arithmetic  1.32 us (1%)
    all_to_all x1, waiting for transfers between devices, per_device(): lax.all_to_all(outgoing, ('feed', 'tm'), split_axis=0, concat_axis=0, til...  53.5 us
    pallas_call x1, Pallas kernels, grams(): pl.pallas_call(functools.partial(gram_kernel, feeds, 1.0 / math.sqrt(fram...  12.1 us
    all_to_all x1, starting transfers between devices, per_device(): lax.all_to_all(outgoing, ('feed', 'tm'), split_axis=0, concat_axis=0, til...  11.1 us
    pallas_call x1, Pallas kernels, head(): pl.pallas_call(head_kernel, in_specs=[pl.BlockSpec(memory_space=pltpu.HBM...  9.77 us
    ppermute x1, starting transfers between devices, per_device(): halo = lax.ppermute(last, 'tm', [(t, t + 1) for t in range(times - 1)])  3.97 us
    pallas_call x1, Pallas kernels, tail(): pl.pallas_call(tail_kernel, in_specs=[pl.BlockSpec(memory_space=pltpu.VME...  2.77 us
  transfers between devices with their start and end apart: 2, of which 1 were waited for; matrix products, arithmetic and copies ran while one was open for 0% of the time, Pallas kernels for 10%

profile of v4, /device:TPU:1, one launch (start us, length us, event | category | flops | bytes accessed | tf_op | source)
XLA Modules:
  0.0 94.9 jit_solution(5880493015986355383)
XLA Ops:
  0.0 1.2 %slice_convert_fusion = bf16[32,6144]{1,0:T(8,128)(2,1)S(1)} fusion(s32[32,65536]{1,0:T(8,128)} %samples_ref.1), kind=kLoop, calls=%fused_computation.2 | loop fusion | flops 196608 | bytes 1179648 | tf_op jit(solution)/shard_map/convert
  1.2 4.0 %collective-permute-start = (bf16[32,6144]{1,0:T(8,128)(2,1)S(1)}, bf16[32,6144]{1,0:T(8,128)(2,1)S(1)}, u32[]{:S(2)}, u32[]{:S(2)}) collective-permute-start(bf16[32,6144]{1,0:T(8,128)(2,1)S(1)} %slice_convert_fusion), channel_id=1, source_target_pairs={{0,1},{1,2},{2,3},{3,4},{4,5},{5,6},{6,7},{8,9},{9,10},{10,11},{11... | collective-permute-start | bytes 1179656 | tf_op jit(solution)/shard_map/ppermute | solution.py:488
  5.2 9.8 %head.1 = (bf16[128,4,4,8,128]{4,3,2,1,0:T(8,128)(2,1)}, bf16[256,2048]{1,0:T(8,128)(2,1)S(1)}, s32[32,6144]{1,0:T(8,128)S(1)}, f32[4,2048]{1,0:T(4,128)S(1)}, bf16[1040,2048]{1,0:T(8,128)(2,1)S(1)}) custom-call(s32[32,65536]{1,0:T(8,128)} %samples_ref.1, f32[4,2048]{1,0:T(4,128)} %constant.33.clone.curve_ref, bf16[1040,2048]{1,0:T(8,128)(2,1)} %constant.34.clone.table_ref), custom_call_target="tpu_custom_call" | custom-call | flops 3271557120 | bytes 12648448 | tf_op jit(solution)/shard_map/head/pallas_call | solution.py:242
  14.9 0.0 collective-permute-done.halo_ref
  14.9 2.8 %tail.1 = bf16[128,4,4,8,128]{4,3,2,1,0:T(8,128)(2,1)} custom-call(s32[32,6144]{1,0:T(8,128)S(1)} %get-tuple-element.10.begin_ref, bf16[32,6144]{1,0:T(8,128)(2,1)S(1)} %collective-permute-done.halo_ref, bf16[256,2048]{1,0:T(8,128)(2,1)S(1)} %get-tuple-element.11.first_ref, ...), custom_call_target="tpu_custom_call", output_to_operand_aliasing={{}: (5, {})} | custom-call | flops 1090519040 | bytes 4259840 | tf_op jit(solution)/shard_map/tail/pallas_call | solution.py:311
  17.7 0.0 copy-start
  17.7 11.1 %all-to-all-start = ((bf16[128,4,4,8,128]{4,3,2,1,0:T(8,128)(2,1)}), bf16[128,4,4,8,128]{4,3,2,1,0:T(8,128)(2,1)}, u32[]{:S(2)}, u32[]{:S(2)}) async-start(bf16[128,4,4,8,128]{4,3,2,1,0:T(8,128)(2,1)} %tail.1), calls=%async_computation | async-start | bytes 8388608 | tf_op jit(solution)/shard_map/all_to_all | solution.py:495
  28.9 0.0 copy-done
  28.9 0.2 fusion.place_ref
  29.0 53.5 %all-to-all-done.x_ref = bf16[128,4,4,8,128]{4,3,2,1,0:T(8,128)(2,1)} async-done(((bf16[128,4,4,8,128]{4,3,2,1,0:T(8,128)(2,1)}), bf16[128,4,4,8,128]{4,3,2,1,0:T(8,128)(2,1)}, u32[]{:S(2)}, u32[]{:S(2)}) %all-to-all-start) | async-done | bytes 4194336 | tf_op jit(solution)/shard_map/all_to_all | solution.py:495
  82.6 12.1 %gram.1 = f32[8,2,512,512]{3,2,1,0:T(8,128)} custom-call(s32[1]{0:T(128)} %bitcast.upper_ref, bf16[128,4,4,8,128]{4,3,2,1,0:T(8,128)(2,1)} %all-to-all-done.x_ref, bf16[512,512]{1,0:T(8,128)(2,1)S(1)} %fusion.place_ref), custom_call_target="tpu_custom_call" | custom-call | flops 6442450944 | bytes 20971520 | tf_op jit(solution)/shard_map/gram/pallas_call | solution.py:449
Async XLA Ops:
  1.2 13.8 %collective-permute-start = (bf16[32,6144]{1,0:T(8,128)(2,1)S(1)}, bf16[32,6144]{1,0:T(8,128)(2,1)S(1)}, u32[]{:S(2)}, u32[]{:S(2)}) collective-permute-start(bf16[32,6144]{1,0:T(8,128)(2,1)S(1)} %slice_convert_fusion), channel_id=1, source_target_pairs={{0,1},{1,2},{2,3},{3,4},{4,5},{5,6},{6,7},{8,9},{9,10},{10,11},{11... | collective-permute-start | bytes 1179656 | tf_op jit(solution)/shard_map/ppermute | solution.py:488
  17.7 11.2 %copy-start = (s32[512]{0:T(512)S(1)}, s32[512]{0:T(512)}, u32[]{:S(2)}) copy-start(s32[512]{0:T(512)} %param.5) | copy-start | bytes 6148
  17.7 64.8 %all-to-all-start = ((bf16[128,4,4,8,128]{4,3,2,1,0:T(8,128)(2,1)}), bf16[128,4,4,8,128]{4,3,2,1,0:T(8,128)(2,1)}, u32[]{:S(2)}, u32[]{:S(2)}) async-start(bf16[128,4,4,8,128]{4,3,2,1,0:T(8,128)(2,1)} %tail.1), calls=%async_computation | async-start | bytes 8388608 | tf_op jit(solution)/shard_map/all_to_all | solution.py:495

commit v5 on v4

--- a/solution.py
+++ b/solution.py
@@ -381,64 +381,52 @@
     z_ref[inputs:, frames:] = (-z[:, :frames]).astype(jnp.bfloat16)
 
 
-def correlate(z_ref, out_ref, norm):
+def correlate(z_ref, out_ref, norm, r):
     inputs = z_ref.shape[1]
-    value = norm * product(z_ref[...], z_ref[:inputs])
-    out_ref[0] = value[:inputs]
-    out_ref[1] = value[inputs:]
+    part = slice(r * inputs, (r + 1) * inputs)
+    out_ref[r] = norm * product(z_ref[part], z_ref[:inputs])
 
 
 def gram_kernel(
-    feeds, norm, upper_ref, x_ref, place_ref, out_ref, held_ref, wide_ref, turned0_ref, turned1_ref,
-    z0_ref, z1_ref, done0_ref, done1_ref, in_sems, out_sems,
+    feeds, norm, upper_ref, x_ref, place_ref, out_ref, held_ref, wide_ref,
+    turned0_ref, turned1_ref, z0_ref, z1_ref, done_ref, in_sems, out_sems,
 ):
-    turned, z, done = (turned0_ref, turned1_ref), (z0_ref, z1_ref), (done0_ref, done1_ref)
+    turned, z = (turned0_ref, turned1_ref), (z0_ref, z1_ref)
     pairs = x_ref.shape[1]
+    channels = PAIR * pairs
 
     def fetch(pair):
         return pltpu.make_async_copy(x_ref.at[:, pair], held_ref.at[pair], in_sems.at[pair])
 
-    def send(pair, parity):
-        low, high = (pair, PAIR * pairs - pair)
-        first = upper_ref[0] == parity
-        local = jnp.where(pair == 0, parity * pairs, jnp.where(first, low, high))
-        return pltpu.make_async_copy(done[parity], out_ref.at[local], out_sems.at[parity])
-
-    def phase(pair, parity, third=True, second=True, first=True, wait=True, wait_more=True):
-        if first and parity == 0:
-            fetch(pair).wait()
-            if not wait_more:
-                for later in range(1, pairs):
-                    fetch(later).start()
-        if third:
-            if wait:
-                send(pair - 2, parity).wait()
-            correlate(z[parity], done[parity], norm)
-        if second:
-            order(turned[1 - parity], place_ref, z[1 - parity])
-        if first:
-            if parity == 0:
-                spread(held_ref[pair], wide_ref)
-            arrange(wide_ref, turned[parity], parity, feeds)
-        if third:
-            send(pair - 1, parity).start()
+    def send(slot, r):
+        low = SLOTS[slot]
+        high = low if slot < PAIR else channels - low
+        local = jnp.where(upper_ref[0] == 0, low, high)
+        return pltpu.make_async_copy(
+            done_ref.at[slot, r], out_ref.at[local, r], out_sems.at[slot, r]
+        )
 
     fetch(0).start()
-    phase(0, 0, third=False, second=False, wait_more=False)
-    phase(0, 1, third=False)
-    phase(1, 0, wait=False)
-    phase(1, 1, wait=False)
-
-    def body(pair, _):
-        phase(pair, 0)
-        phase(pair, 1)
-        return 0
-
-    lax.fori_loop(2, pairs, body, 0)
-    phase(pairs, 0, first=False)
-    phase(pairs, 1, second=False, first=False)
-    for parity in range(PAIR):
-        send(pairs - 1, parity).wait()
+    for step in range(channels + 2):
+        now = step % 2
+        if step < channels and step % PAIR == 0:
+            fetch(step // PAIR).wait()
+            if step == 0:
+                for pair in range(1, pairs):
+                    fetch(pair).start()
+        if step > 1:
+            for r in range(2):
+                correlate(z[now], done_ref.at[step - 2], norm, r)
+                send(step - 2, r).start()
+        if 0 < step <= channels:
+            order(turned[1 - now], place_ref, z[1 - now])
+        if step < channels:
+            if step % PAIR == 0:
+                spread(held_ref[step // PAIR], wide_ref)
+            arrange(wide_ref, turned[now], step % PAIR, feeds)
+    for slot in range(channels):
+        for r in range(2):
+            send(slot, r).wait()
 
 
 def grams(upper, incoming, place, feeds):
@@ -462,10 +450,9 @@
             pltpu.VMEM((2 * frames, inputs), jnp.bfloat16),
             pltpu.VMEM((2 * inputs, 2 * frames), jnp.bfloat16),
             pltpu.VMEM((2 * inputs, 2 * frames), jnp.bfloat16),
-            pltpu.VMEM((2, inputs, inputs), jnp.float32),
-            pltpu.VMEM((2, inputs, inputs), jnp.float32),
+            pltpu.VMEM((channels, 2, inputs, inputs), jnp.float32),
             pltpu.SemaphoreType.DMA((pairs,)),
-            pltpu.SemaphoreType.DMA((PAIR,)),
+            pltpu.SemaphoreType.DMA((channels, 2)),
         ],
         compiler_params=pltpu.CompilerParams(vmem_limit_bytes=40 * MIB),
         cost_estimate=pl.CostEstimate(
@@ -474,7 +461,7 @@
             transcendentals=0,
         ),
         name="gram",
-    )(upper, *in_hbm(incoming), place)
+    )(upper, *in_hbm(incoming), *in_vmem(place))
 
 
 def per_device(samples, input_map):

time: 95.2 us -> 94.5 us (level)
  no operation moved by 1% of the time
where the time goes in v5:
time: 94.5 us; the launch traced here: 94.2 us
  waiting for transfers between devices  53.5 us (57%)
  Pallas kernels  24 us (25%)
  starting transfers between devices  15.1 us (16%)
  other arithmetic  1.32 us (1%)
    all_to_all x1, waiting for transfers between devices, per_device(): lax.all_to_all(outgoing, ('feed', 'tm'), split_axis=0, concat_axis=0, til...  53.5 us
    pallas_call x1, Pallas kernels, grams(): pl.pallas_call(functools.partial(gram_kernel, feeds, 1.0 / math.sqrt(fram...  11.5 us
    all_to_all x1, starting transfers between devices, per_device(): lax.all_to_all(outgoing, ('feed', 'tm'), split_axis=0, concat_axis=0, til...  11.1 us
    pallas_call x1, Pallas kernels, head(): pl.pallas_call(head_kernel, in_specs=[pl.BlockSpec(memory_space=pltpu.HBM...  9.77 us
    ppermute x1, starting transfers between devices, per_device(): halo = lax.ppermute(last, 'tm', [(t, t + 1) for t in range(times - 1)])  3.97 us
    pallas_call x1, Pallas kernels, tail(): pl.pallas_call(tail_kernel, in_specs=[pl.BlockSpec(memory_space=pltpu.VME...  2.77 us
  transfers between devices with their start and end apart: 2, of which 1 were waited for; matrix products, arithmetic and copies ran while one was open for 0% of the time, Pallas kernels for 10%

profile of v5, /device:TPU:1, one launch (start us, length us, event | category | flops | bytes accessed | tf_op | source)
XLA Modules:
  0.0 94.2 jit_solution(3028137588620141686)
XLA Ops:
  0.0 1.2 %slice_convert_fusion = bf16[32,6144]{1,0:T(8,128)(2,1)S(1)} fusion(s32[32,65536]{1,0:T(8,128)} %samples_ref.1), kind=kLoop, calls=%fused_computation.2 | loop fusion | flops 196608 | bytes 1179648 | tf_op jit(solution)/shard_map/convert
  1.2 4.0 %collective-permute-start = (bf16[32,6144]{1,0:T(8,128)(2,1)S(1)}, bf16[32,6144]{1,0:T(8,128)(2,1)S(1)}, u32[]{:S(2)}, u32[]{:S(2)}) collective-permute-start(bf16[32,6144]{1,0:T(8,128)(2,1)S(1)} %slice_convert_fusion), channel_id=1, source_target_pairs={{0,1},{1,2},{2,3},{3,4},{4,5},{5,6},{6,7},{8,9},{9,10},{10,11},{11... | collective-permute-start | bytes 1179656 | tf_op jit(solution)/shard_map/ppermute | solution.py:475
  5.2 9.8 %head.1 = (bf16[128,4,4,8,128]{4,3,2,1,0:T(8,128)(2,1)}, bf16[256,2048]{1,0:T(8,128)(2,1)S(1)}, s32[32,6144]{1,0:T(8,128)S(1)}, f32[4,2048]{1,0:T(4,128)S(1)}, bf16[1040,2048]{1,0:T(8,128)(2,1)S(1)}) custom-call(s32[32,65536]{1,0:T(8,128)} %samples_ref.1, f32[4,2048]{1,0:T(4,128)} %constant.33.clone.curve_ref, bf16[1040,2048]{1,0:T(8,128)(2,1)} %constant.34.clone.table_ref), custom_call_target="tpu_custom_call" | custom-call | flops 3271557120 | bytes 12648448 | tf_op jit(solution)/shard_map/head/pallas_call | solution.py:242
  14.9 0.0 collective-permute-done.halo_ref
  14.9 2.8 %tail.1 = bf16[128,4,4,8,128]{4,3,2,1,0:T(8,128)(2,1)} custom-call(s32[32,6144]{1,0:T(8,128)S(1)} %get-tuple-element.10.begin_ref, bf16[32,6144]{1,0:T(8,128)(2,1)S(1)} %collective-permute-done.halo_ref, bf16[256,2048]{1,0:T(8,128)(2,1)S(1)} %get-tuple-element.11.first_ref, ...), custom_call_target="tpu_custom_call", output_to_operand_aliasing={{}: (5, {})} | custom-call | flops 1090519040 | bytes 4259840 | tf_op jit(solution)/shard_map/tail/pallas_call | solution.py:311
  17.7 0.0 copy-start
  17.7 11.1 %all-to-all-start = ((bf16[128,4,4,8,128]{4,3,2,1,0:T(8,128)(2,1)}), bf16[128,4,4,8,128]{4,3,2,1,0:T(8,128)(2,1)}, u32[]{:S(2)}, u32[]{:S(2)}) async-start(bf16[128,4,4,8,128]{4,3,2,1,0:T(8,128)(2,1)} %tail.1), calls=%async_computation | async-start | bytes 8388608 | tf_op jit(solution)/shard_map/all_to_all | solution.py:482
  28.9 0.0 copy-done
  28.9 0.2 fusion.place_ref
  29.0 53.5 %all-to-all-done.x_ref = bf16[128,4,4,8,128]{4,3,2,1,0:T(8,128)(2,1)} async-done(((bf16[128,4,4,8,128]{4,3,2,1,0:T(8,128)(2,1)}), bf16[128,4,4,8,128]{4,3,2,1,0:T(8,128)(2,1)}, u32[]{:S(2)}, u32[]{:S(2)}) %all-to-all-start) | async-done | bytes 4194336 | tf_op jit(solution)/shard_map/all_to_all | solution.py:482
  82.6 11.5 %gram.1 = f32[8,2,512,512]{3,2,1,0:T(8,128)} custom-call(s32[1]{0:T(128)} %bitcast.upper_ref, bf16[128,4,4,8,128]{4,3,2,1,0:T(8,128)(2,1)} %all-to-all-done.x_ref, bf16[512,512]{1,0:T(8,128)(2,1)S(1)} %fusion.place_ref), custom_call_target="tpu_custom_call" | custom-call | flops 6442450944 | bytes 20971520 | tf_op jit(solution)/shard_map/gram/pallas_call | solution.py:437
Async XLA Ops:
  1.2 13.8 %collective-permute-start = (bf16[32,6144]{1,0:T(8,128)(2,1)S(1)}, bf16[32,6144]{1,0:T(8,128)(2,1)S(1)}, u32[]{:S(2)}, u32[]{:S(2)}) collective-permute-start(bf16[32,6144]{1,0:T(8,128)(2,1)S(1)} %slice_convert_fusion), channel_id=1, source_target_pairs={{0,1},{1,2},{2,3},{3,4},{4,5},{5,6},{6,7},{8,9},{9,10},{10,11},{11... | collective-permute-start | bytes 1179656 | tf_op jit(solution)/shard_map/ppermute | solution.py:475
  17.7 11.2 %copy-start = (s32[512]{0:T(512)S(1)}, s32[512]{0:T(512)}, u32[]{:S(2)}) copy-start(s32[512]{0:T(512)} %param.5) | copy-start | bytes 6148
  17.7 64.8 %all-to-all-start = ((bf16[128,4,4,8,128]{4,3,2,1,0:T(8,128)(2,1)}), bf16[128,4,4,8,128]{4,3,2,1,0:T(8,128)(2,1)}, u32[]{:S(2)}, u32[]{:S(2)}) async-start(bf16[128,4,4,8,128]{4,3,2,1,0:T(8,128)(2,1)} %tail.1), calls=%async_computation | async-start | bytes 8388608 | tf_op jit(solution)/shard_map/all_to_all | solution.py:482

commit v6 on v5

--- a/solution.py
+++ b/solution.py
@@ -381,10 +381,18 @@
     z_ref[inputs:, frames:] = (-z[:, :frames]).astype(jnp.bfloat16)
 
 
-def correlate(z_ref, out_ref, norm, r):
+def correlate(z_ref, out_ref, norm):
     inputs = z_ref.shape[1]
-    part = slice(r * inputs, (r + 1) * inputs)
-    out_ref[r] = norm * product(z_ref[part], z_ref[:inputs])
+    half = inputs // 2
+    left = norm * product(z_ref[...], z_ref[:half])
+    below = jnp.concatenate([z_ref[half:inputs], z_ref[inputs + half :]], axis=0)
+    right = norm * product(below, z_ref[half:inputs])
+    for r in range(2):
+        corner = left[r * inputs + half : (r + 1) * inputs]
+        out_ref[r, :half, :half] = left[r * inputs : r * inputs + half]
+        out_ref[r, half:, :half] = corner
+        out_ref[r, half:, half:] = right[r * half : (r + 1) * half]
+        out_ref[r, :half, half:] = corner.T if r == 0 else -corner.T
 
 
 def gram_kernel(
@@ -415,8 +423,8 @@
                 for pair in range(1, pairs):
                     fetch(pair).start()
         if step > 1:
+            correlate(z[now], done_ref.at[step - 2], norm)
             for r in range(2):
-                correlate(z[now], done_ref.at[step - 2], norm, r)
                 send(step - 2, r).start()
         if 0 < step <= channels:
             order(turned[1 - now], place_ref, z[1 - now])

time: 94.5 us -> 94.5 us (level)
  no operation moved by 1% of the time
where the time goes in v6:
time: 94.5 us; the launch traced here: 94.2 us
  waiting for transfers between devices  53.5 us (57%)
  Pallas kernels  24 us (25%)
  starting transfers between devices  15.1 us (16%)
  other arithmetic  1.32 us (1%)
    all_to_all x1, waiting for transfers between devices, per_device(): lax.all_to_all(outgoing, ('feed', 'tm'), split_axis=0, concat_axis=0, til...  53.5 us
    pallas_call x1, Pallas kernels, grams(): pl.pallas_call(functools.partial(gram_kernel, feeds, 1.0 / math.sqrt(fram...  11.4 us
    all_to_all x1, starting transfers between devices, per_device(): lax.all_to_all(outgoing, ('feed', 'tm'), split_axis=0, concat_axis=0, til...  11.1 us
    pallas_call x1, Pallas kernels, head(): pl.pallas_call(head_kernel, in_specs=[pl.BlockSpec(memory_space=pltpu.HBM...  9.77 us
    ppermute x1, starting transfers between devices, per_device(): halo = lax.ppermute(last, 'tm', [(t, t + 1) for t in range(times - 1)])  3.97 us
    pallas_call x1, Pallas kernels, tail(): pl.pallas_call(tail_kernel, in_specs=[pl.BlockSpec(memory_space=pltpu.VME...  2.77 us
  transfers between devices with their start and end apart: 2, of which 1 were waited for; matrix products, arithmetic and copies ran while one was open for 0% of the time, Pallas kernels for 10%

profile of v6, /device:TPU:1, one launch (start us, length us, event | category | flops | bytes accessed | tf_op | source)
XLA Modules:
  0.0 94.2 jit_solution(14090954388548097728)
XLA Ops:
  0.0 1.2 %slice_convert_fusion = bf16[32,6144]{1,0:T(8,128)(2,1)S(1)} fusion(s32[32,65536]{1,0:T(8,128)} %samples_ref.1), kind=kLoop, calls=%fused_computation.2 | loop fusion | flops 196608 | bytes 1179648 | tf_op jit(solution)/shard_map/convert
  1.2 4.0 %collective-permute-start = (bf16[32,6144]{1,0:T(8,128)(2,1)S(1)}, bf16[32,6144]{1,0:T(8,128)(2,1)S(1)}, u32[]{:S(2)}, u32[]{:S(2)}) collective-permute-start(bf16[32,6144]{1,0:T(8,128)(2,1)S(1)} %slice_convert_fusion), channel_id=1, source_target_pairs={{0,1},{1,2},{2,3},{3,4},{4,5},{5,6},{6,7},{8,9},{9,10},{10,11},{11... | collective-permute-start | bytes 1179656 | tf_op jit(solution)/shard_map/ppermute | solution.py:483
  5.2 9.8 %head.1 = (bf16[128,4,4,8,128]{4,3,2,1,0:T(8,128)(2,1)}, bf16[256,2048]{1,0:T(8,128)(2,1)S(1)}, s32[32,6144]{1,0:T(8,128)S(1)}, f32[4,2048]{1,0:T(4,128)S(1)}, bf16[1040,2048]{1,0:T(8,128)(2,1)S(1)}) custom-call(s32[32,65536]{1,0:T(8,128)} %samples_ref.1, f32[4,2048]{1,0:T(4,128)} %constant.33.clone.curve_ref, bf16[1040,2048]{1,0:T(8,128)(2,1)} %constant.34.clone.table_ref), custom_call_target="tpu_custom_call" | custom-call | flops 3271557120 | bytes 12648448 | tf_op jit(solution)/shard_map/head/pallas_call | solution.py:242
  14.9 0.0 collective-permute-done.halo_ref
  14.9 2.8 %tail.1 = bf16[128,4,4,8,128]{4,3,2,1,0:T(8,128)(2,1)} custom-call(s32[32,6144]{1,0:T(8,128)S(1)} %get-tuple-element.10.begin_ref, bf16[32,6144]{1,0:T(8,128)(2,1)S(1)} %collective-permute-done.halo_ref, bf16[256,2048]{1,0:T(8,128)(2,1)S(1)} %get-tuple-element.11.first_ref, ...), custom_call_target="tpu_custom_call", output_to_operand_aliasing={{}: (5, {})} | custom-call | flops 1090519040 | bytes 4259840 | tf_op jit(solution)/shard_map/tail/pallas_call | solution.py:311
  17.7 0.0 copy-start
  17.7 11.1 %all-to-all-start = ((bf16[128,4,4,8,128]{4,3,2,1,0:T(8,128)(2,1)}), bf16[128,4,4,8,128]{4,3,2,1,0:T(8,128)(2,1)}, u32[]{:S(2)}, u32[]{:S(2)}) async-start(bf16[128,4,4,8,128]{4,3,2,1,0:T(8,128)(2,1)} %tail.1), calls=%async_computation | async-start | bytes 8388608 | tf_op jit(solution)/shard_map/all_to_all | solution.py:490
  28.9 0.0 copy-done
  28.9 0.2 fusion.place_ref
  29.0 53.5 %all-to-all-done.x_ref = bf16[128,4,4,8,128]{4,3,2,1,0:T(8,128)(2,1)} async-done(((bf16[128,4,4,8,128]{4,3,2,1,0:T(8,128)(2,1)}), bf16[128,4,4,8,128]{4,3,2,1,0:T(8,128)(2,1)}, u32[]{:S(2)}, u32[]{:S(2)}) %all-to-all-start) | async-done | bytes 4194336 | tf_op jit(solution)/shard_map/all_to_all | solution.py:490
  82.6 11.4 %gram.1 = f32[8,2,512,512]{3,2,1,0:T(8,128)} custom-call(s32[1]{0:T(128)} %bitcast.upper_ref, bf16[128,4,4,8,128]{4,3,2,1,0:T(8,128)(2,1)} %all-to-all-done.x_ref, bf16[512,512]{1,0:T(8,128)(2,1)S(1)} %fusion.place_ref), custom_call_target="tpu_custom_call" | custom-call | flops 6442450944 | bytes 20971520 | tf_op jit(solution)/shard_map/gram/pallas_call | solution.py:445
Async XLA Ops:
  1.2 13.8 %collective-permute-start = (bf16[32,6144]{1,0:T(8,128)(2,1)S(1)}, bf16[32,6144]{1,0:T(8,128)(2,1)S(1)}, u32[]{:S(2)}, u32[]{:S(2)}) collective-permute-start(bf16[32,6144]{1,0:T(8,128)(2,1)S(1)} %slice_convert_fusion), channel_id=1, source_target_pairs={{0,1},{1,2},{2,3},{3,4},{4,5},{5,6},{6,7},{8,9},{9,10},{10,11},{11... | collective-permute-start | bytes 1179656 | tf_op jit(solution)/shard_map/ppermute | solution.py:483
  17.7 11.2 %copy-start = (s32[512]{0:T(512)S(1)}, s32[512]{0:T(512)}, u32[]{:S(2)}) copy-start(s32[512]{0:T(512)} %param.5) | copy-start | bytes 6148
  17.7 64.8 %all-to-all-start = ((bf16[128,4,4,8,128]{4,3,2,1,0:T(8,128)(2,1)}), bf16[128,4,4,8,128]{4,3,2,1,0:T(8,128)(2,1)}, u32[]{:S(2)}, u32[]{:S(2)}) async-start(bf16[128,4,4,8,128]{4,3,2,1,0:T(8,128)(2,1)} %tail.1), calls=%async_computation | async-start | bytes 8388608 | tf_op jit(solution)/shard_map/all_to_all | solution.py:490
